TPU v7x, 32 devices: a whole 2x2x4 slice. The times are simulated.
32 devices in a mesh: dp: 4 (over y, core), ctx: 2 (over x), tensor: 4 (over z).
Axes of the slice: x: 2, y: 2, z: 4, core: 2. Of those that a mesh axis runs over, the one named last changes fastest.
Arguments:
- inputs: bfloat16 [4, 2048, 2048], P('dp', 'ctx'), may hold values from -6 to 6
- cotangent: bfloat16 [4, 2048, 2048], P('dp', 'ctx'), may hold values from -6 to 6
- skip_mask: int32 [4], P('dp'), may hold values from 0 to 1, as said below
- group_ids: int32 [4], P('dp'), may hold values from 0 to 1, as said below
- span_order: int32 [4, 4], P('dp'), may hold values from 0 to 3, each once within a row
- exit_scale: float32 [2], replicated, may hold values from 0.5 to 2
- attn_gain: float32 [2048], replicated, may hold values from 0.5 to 1.5
- ffn_gain: float32 [2048], replicated, may hold values from 0.5 to 1.5
- w_query: bfloat16 [2048, 2048], P(None, 'tensor'), may hold values from -0.125 to 0.125
- w_key: bfloat16 [2048, 1024], P(None, 'tensor'), may hold values from -0.125 to 0.125
- w_value: bfloat16 [2048, 1024], P(None, 'tensor'), may hold values from -0.125 to 0.125
- w_output: bfloat16 [2048, 2048], P('tensor'), may hold values from -2 to 2
- w_gate: bfloat16 [2048, 5632], P(None, 'tensor'), may hold values from -0.125 to 0.125
- w_up: bfloat16 [2048, 5632], P(None, 'tensor'), may hold values from -0.125 to 0.125
- w_down: bfloat16 [5632, 2048], P('tensor'), may hold values from -0.078125 to 0.078125
Outputs:
- output: bfloat16 [4, 2048, 2048], P('dp', 'ctx')
- input_grad: float32 [4, 2048, 2048], P('dp', 'ctx')
- attn_gain_grad: float32 [2048], replicated
- ffn_gain_grad: float32 [2048], replicated
- query_grad: float32 [2048, 2048], P(None, 'tensor')
- key_grad: float32 [2048, 1024], P(None, 'tensor')
- value_grad: float32 [2048, 1024], P(None, 'tensor')
- out_proj_grad: float32 [2048, 2048], P('tensor')
- gate_grad: float32 [2048, 5632], P(None, 'tensor')
- up_grad: float32 [2048, 5632], P(None, 'tensor')
- down_grad: float32 [5632, 2048], P('tensor')
Inputs may be any that keep to these rules, and one draw needn't show every extreme that they name: `skip_mask`: at least one sequence runs the block and at least one skips it. `group_ids`: both groups are present.
All inputs are finite; a program needn't handle non-finite values.
Results may differ from a plain program's by a relative error of at most 0.014.
Values may be sent and summed in bfloat16 or wider, within the bound.
A program may use at most 320 MiB of HBM per device.

v0:
```python
import jax
import jax.numpy as jnp
from jax import lax
from jax.sharding import PartitionSpec as P

HEAD_DIM = 128


EPSILON = 1e-05
NEG_BIG = -1e30


def sequence_positions(order_row, length):
    spans = order_row.shape[0]
    stride = length // spans
    places = jnp.arange(length, dtype=jnp.int32)
    onehot = (places // stride)[:, None] == jnp.arange(spans, dtype=jnp.int32)[None, :]
    starts = jnp.sum(jnp.where(onehot, order_row[None, :], 0), axis=1)
    return starts * stride + places % stride


def rotary_tables(positions):
    inverse = 1.0 / 10000.0 ** (jnp.arange(0, HEAD_DIM, 2, dtype=jnp.float32) / HEAD_DIM)
    angle = positions.astype(jnp.float32)[:, None] * inverse[None, :]
    return (jnp.cos(angle), jnp.sin(angle))


def rotate(field, cosine, sine):
    half = field.shape[-1] // 2
    leading, trailing = (field[..., :half], field[..., half:])
    cosine, sine = (cosine[:, None, :], sine[:, None, :])
    return jnp.concatenate(
        [leading * cosine - trailing * sine, trailing * cosine + leading * sine], axis=-1
    )


def rotate_back(grad, cosine, sine):
    half = grad.shape[-1] // 2
    leading, trailing = (grad[..., :half], grad[..., half:])
    cosine, sine = (cosine[:, None, :], sine[:, None, :])
    return jnp.concatenate(
        [leading * cosine + trailing * sine, trailing * cosine - leading * sine], axis=-1
    )


def block_scores(query_block, keys, place_block, key_places, factor):
    scores = (
        jnp.einsum("bhgd,lhd->hgbl", query_block, keys, preferred_element_type=jnp.float32) * factor
    )
    allowed = key_places[None, :] <= place_block[:, None]
    return jnp.where(allowed[None, None], scores, NEG_BIG)


def attend(queries, keys, values, query_places, key_places, block, factor):
    count = queries.shape[0] // block
    query_blocks = queries.reshape((count, block) + queries.shape[1:])
    place_blocks = query_places.reshape(count, block)

    def one_block(packed):
        query_block, place_block = packed
        scores = block_scores(query_block, keys, place_block, key_places, factor)
        top = jnp.max(scores, axis=-1, keepdims=True)
        weights = jnp.exp(scores - top)
        total = jnp.sum(weights, axis=-1, keepdims=True)
        probs = weights / total
        mixed = jnp.einsum(
            "hgbl,lhd->bhgd", probs.astype(jnp.bfloat16), values, preferred_element_type=jnp.float32
        )
        return (mixed.astype(jnp.bfloat16), (top + jnp.log(total))[..., 0])

    mixed, log_total = lax.map(one_block, (query_blocks, place_blocks))
    return (mixed.reshape(queries.shape), log_total)


def attend_back(queries, keys, values, dmixed, log_total, query_places, key_places, block, factor):
    count = queries.shape[0] // block
    query_blocks = queries.reshape((count, block) + queries.shape[1:])
    dmix_blocks = dmixed.reshape((count, block) + dmixed.shape[1:])
    place_blocks = query_places.reshape(count, block)

    def one_block(carry, packed):
        dkeys, dvalues = carry
        query_block, dmix_block, total_block, place_block = packed
        scores = block_scores(query_block, keys, place_block, key_places, factor)
        probs = jnp.exp(scores - total_block[..., None])
        dprobs = jnp.einsum(
            "bhgd,lhd->hgbl", dmix_block, values, preferred_element_type=jnp.float32
        )
        dscore = probs * (dprobs - jnp.sum(probs * dprobs, axis=-1, keepdims=True))
        dscore = dscore.astype(jnp.bfloat16)
        dquery = (
            jnp.einsum("hgbl,lhd->bhgd", dscore, keys, preferred_element_type=jnp.float32) * factor
        )
        dkeys = (
            dkeys
            + jnp.einsum("hgbl,bhgd->lhd", dscore, query_block, preferred_element_type=jnp.float32)
            * factor
        )
        dvalues = dvalues + jnp.einsum(
            "hgbl,bhgd->lhd",
            probs.astype(jnp.bfloat16),
            dmix_block,
            preferred_element_type=jnp.float32,
        )
        return ((dkeys, dvalues), dquery)

    empty = jnp.zeros(keys.shape, jnp.float32)
    (dkeys, dvalues), dquery = lax.scan(
        one_block, (empty, empty), (query_blocks, dmix_blocks, log_total, place_blocks)
    )
    return (dquery.reshape(queries.shape), dkeys, dvalues)


def contract_rows(left, right):
    return jnp.einsum("rd,rf->df", left, right, preferred_element_type=jnp.float32)


def contract_cols(left, right):
    return jnp.einsum("rc,dc->rd", left, right, preferred_element_type=jnp.float32)


def norm_back(dnormed, unit, inverse, gain):
    scaled = dnormed * gain
    return inverse * (scaled - unit * jnp.mean(scaled * unit, axis=-1, keepdims=True))


def per_device(
    inputs,
    cotangent,
    skip_mask,
    group_ids,
    span_order,
    exit_scale,
    attn_gain,
    ffn_gain,
    w_query,
    w_key,
    w_value,
    w_output,
    w_gate,
    w_up,
    w_down,
):
    seq_count, local_len, width = inputs.shape
    full_len = local_len * lax.axis_size("ctx")
    row_total = seq_count * local_len
    head_local = w_query.shape[1] // HEAD_DIM
    kv_local = w_key.shape[1] // HEAD_DIM
    group_size = head_local // kv_local
    block = min(512, local_len)
    factor = HEAD_DIM ** (-0.5)
    offset = lax.axis_index("ctx") * local_len
    key_places = [sequence_positions(span_order[0], full_len)]
    query_places = [lax.dynamic_slice_in_dim(key_places[0], offset, local_len)]
    cosine, sine = rotary_tables(query_places[0])
    keep_rows = jnp.repeat(skip_mask.astype(jnp.float32), local_len)[:, None]
    chosen = jnp.where(group_ids == 1, exit_scale[1], exit_scale[0])
    scale_rows = jnp.repeat(chosen, local_len)[:, None]
    flat = inputs.reshape(row_total, width).astype(jnp.float32)
    inv_one = lax.rsqrt(jnp.mean(flat * flat, axis=-1, keepdims=True) + EPSILON)
    unit_one = flat * inv_one
    normed_one = (unit_one * attn_gain).astype(jnp.bfloat16)
    q_proj = jnp.dot(normed_one, w_query, preferred_element_type=jnp.float32).reshape(
        row_total, head_local, HEAD_DIM
    )
    queries = rotate(q_proj, cosine, sine).astype(jnp.bfloat16)
    k_proj = jnp.dot(normed_one, w_key, preferred_element_type=jnp.float32).reshape(
        row_total, kv_local, HEAD_DIM
    )
    keys_local = rotate(k_proj, cosine, sine).astype(jnp.bfloat16)
    values_local = jnp.dot(normed_one, w_value, preferred_element_type=jnp.float32).astype(
        jnp.bfloat16
    )
    kv_shape = (seq_count, local_len, kv_local * HEAD_DIM)
    keys_sent = keys_local.reshape(kv_shape)
    values_sent = values_local.reshape(kv_shape)
    keys_all, values_all = (
        lax.all_gather(keys_sent, "ctx", axis=1, tiled=True),
        lax.all_gather(values_sent, "ctx", axis=1, tiled=True),
    )
    item = 0
    query_seq = queries.reshape(local_len, kv_local, group_size, HEAD_DIM)
    mixed, log_total = attend(
        query_seq,
        keys_all[item].reshape(full_len, kv_local, HEAD_DIM),
        values_all[item].reshape(full_len, kv_local, HEAD_DIM),
        query_places[item],
        key_places[item],
        block,
        factor,
    )
    mixed_parts = mixed.reshape(local_len, head_local * HEAD_DIM)
    total_parts = [log_total]
    dscaled = cotangent.reshape(row_total, width).astype(jnp.float32) * scale_rows
    attn_part = jnp.dot(mixed_parts, w_output, preferred_element_type=jnp.float32)
    attn_branch = lax.psum(attn_part, "tensor")
    hidden_in = flat + attn_branch
    inv_two = lax.rsqrt(jnp.mean(hidden_in * hidden_in, axis=-1, keepdims=True) + EPSILON)
    unit_two = hidden_in * inv_two
    normed_two = (unit_two * ffn_gain).astype(jnp.bfloat16)
    gate = jnp.dot(normed_two, w_gate, preferred_element_type=jnp.float32)
    upward = jnp.dot(normed_two, w_up, preferred_element_type=jnp.float32)
    sigmoid_gate = jax.nn.sigmoid(gate)
    silu_gate = gate * sigmoid_gate
    acted = (silu_gate * upward).astype(jnp.bfloat16)
    dffn = (keep_rows * dscaled).astype(jnp.bfloat16)
    dacted = contract_cols(dffn, w_down)
    dgate = (dacted * upward * sigmoid_gate * (1.0 + gate * (1.0 - sigmoid_gate))).astype(
        jnp.bfloat16
    )
    dupward = (dacted * silu_gate).astype(jnp.bfloat16)
    grad_down = contract_rows(acted, dffn)
    grad_gate = contract_rows(normed_two, dgate)
    grad_up = contract_rows(normed_two, dupward)
    ffn_part = jnp.dot(acted, w_down, preferred_element_type=jnp.float32)
    ffn_branch = lax.psum(ffn_part.astype(jnp.bfloat16), "tensor").astype(jnp.float32)
    output = (flat + keep_rows * (attn_branch + ffn_branch)).astype(jnp.bfloat16)
    dnormed_two = lax.psum(contract_cols(dgate, w_gate) + contract_cols(dupward, w_up), "tensor")
    grad_ffn_gain = jnp.sum(dnormed_two * unit_two, axis=0)
    dhidden = norm_back(dnormed_two, unit_two, inv_two, ffn_gain)
    dattn = (keep_rows * dscaled + dhidden).astype(jnp.bfloat16)
    grad_output = contract_rows(mixed_parts, dattn)
    dmixed_all = contract_cols(dattn, w_output).astype(jnp.bfloat16)
    keys_back, values_back = (keys_all, values_all)
    item = 0
    query_seq = queries.reshape(local_len, kv_local, group_size, HEAD_DIM)
    dmix_seq = dmixed_all.reshape(local_len, kv_local, group_size, HEAD_DIM)
    dquery, dkeys, dvalues = attend_back(
        query_seq,
        keys_back[item].reshape(full_len, kv_local, HEAD_DIM),
        values_back[item].reshape(full_len, kv_local, HEAD_DIM),
        dmix_seq,
        total_parts[item],
        query_places[item],
        key_places[item],
        block,
        factor,
    )
    dquery_parts = dquery.reshape(local_len, head_local, HEAD_DIM)
    dkey_parts = [dkeys.reshape(full_len, kv_local * HEAD_DIM)]
    dvalue_parts = [dvalues.reshape(full_len, kv_local * HEAD_DIM)]
    dkeys_own, dvalues_own = (
        lax.psum_scatter(jnp.stack(dkey_parts), "ctx", scatter_dimension=1, tiled=True),
        lax.psum_scatter(jnp.stack(dvalue_parts), "ctx", scatter_dimension=1, tiled=True),
    )
    dq_proj = (
        rotate_back(dquery_parts, cosine, sine)
        .reshape(row_total, head_local * HEAD_DIM)
        .astype(jnp.bfloat16)
    )
    dk_proj = (
        rotate_back(dkeys_own.reshape(row_total, kv_local, HEAD_DIM), cosine, sine)
        .reshape(row_total, kv_local * HEAD_DIM)
        .astype(jnp.bfloat16)
    )
    dv_proj = dvalues_own.reshape(row_total, kv_local * HEAD_DIM).astype(jnp.bfloat16)
    grad_query = contract_rows(normed_one, dq_proj)
    grad_key = contract_rows(normed_one, dk_proj)
    grad_value = contract_rows(normed_one, dv_proj)
    dnormed_one = lax.psum(
        contract_cols(dq_proj, w_query)
        + contract_cols(dk_proj, w_key)
        + contract_cols(dv_proj, w_value),
        "tensor",
    )
    grad_attn_gain = jnp.sum(dnormed_one * unit_one, axis=0)
    input_grad = dscaled + dhidden + norm_back(dnormed_one, unit_one, inv_one, attn_gain)
    (
        grad_query,
        grad_key,
        grad_value,
        grad_output,
        grad_attn_gain,
        grad_gate,
        grad_up,
        grad_down,
        grad_ffn_gain,
    ) = lax.psum(
        (
            grad_query,
            grad_key,
            grad_value,
            grad_output,
            grad_attn_gain,
            grad_gate,
            grad_up,
            grad_down,
            grad_ffn_gain,
        ),
        ("dp", "ctx"),
    )
    return (
        output.reshape(inputs.shape),
        input_grad.reshape(inputs.shape),
        grad_attn_gain,
        grad_ffn_gain,
        grad_query,
        grad_key,
        grad_value,
        grad_output,
        grad_gate,
        grad_up,
        grad_down,
    )


def solution(mesh):
    in_specs = (
        P("dp", "ctx", None),
        P("dp", "ctx", None),
        P("dp"),
        P("dp"),
        P("dp", None),
        P(),
        P(),
        P(),
        P(None, "tensor"),
        P(None, "tensor"),
        P(None, "tensor"),
        P("tensor", None),
        P(None, "tensor"),
        P(None, "tensor"),
        P("tensor", None),
    )
    out_specs = (
        P("dp", "ctx", None),
        P("dp", "ctx", None),
        P(),
        P(),
        P(None, "tensor"),
        P(None, "tensor"),
        P(None, "tensor"),
        P("tensor", None),
        P(None, "tensor"),
        P(None, "tensor"),
        P("tensor", None),
    )
    return jax.shard_map(
        per_device, mesh=mesh, in_specs=in_specs, out_specs=out_specs, check_vma=False
    )
```

profile of v0, /device:TPU:0, one launch (start us, length us, event | category | flops | bytes accessed | tf_op | source)
XLA Modules:
  0.0 2056.2 jit_solution(14856694012144326580)
XLA Ops:
  46.9 20.3 all-gather.6.cloned.1.call-done
  69.7 34.4 %while.27 = (s32[]{:T(128)}, bf16[2,512,2,2,128]{4,3,2,1,0:T(2,128)(2,1)}, f32[2,2,2,512]{3,2,1,0:T(2,128)S(1)}, s32[2048]{0:T(1024)S(1)}, s32[2,512]{1,0:T(2,12...) while((s32[]{:T(128)}, ...), condition=%wide.region_5.6_spmd, body=%wide.region_2.5_spmd.sunk | while | flops 2199123968 | bytes 71383248 | solution.py:71
  117.0 287.8 %all-reduce.8.cloned.1.call-done = f32[1024,2048]{1,0:T(8,128)} async-done(((f32[1024,2048]{1,0:T(8,128)}), f32[1024,2048]{1,0:T(8,128)}) %all-reduce.8.cloned.1.call-update) | async-done | bytes 8388624 | tf_op jit(solution)/shard_map/psum | solution.py:196
  432.1 15.3 multiply_convert_fusion.1
  457.1 10.9 convolution_add_fusion
  468.2 289.9 %all-reduce.12.cloned.1.call-done = f32[1024,2048]{1,0:T(8,128)} async-done(((f32[1024,2048]{1,0:T(8,128)}), f32[1024,2048]{1,0:T(8,128)}) %all-reduce.12.cloned.1.call-update) | async-done | bytes 8388624 | tf_op jit(solution)/shard_map/psum | solution.py:218
  783.9 145.1 %while.28 = (s32[]{:T(128)}, f32[2048,2,128]{0,2,1:T(8,128)}, f32[2048,2,128]{0,2,1:T(8,128)}, f32[2,512,2,2,128]{1,0,4,3,2:T(2,128)}, bf16[2,512,2,2,128]{4,1,3...) while((s32[]{:T(128)}, f32[2048,2,128]{0,2,1:T(8,128)}, ...), condition=%wide.region_13.14_spmd.clone, body=%wide.region_11.13_spmd.clone.sunk | while | flops 5435553792 | bytes 246487344 | solution.py:108
  802.7 12.5 fusion.177
  815.1 12.2 fusion.178
  836.4 19.7 dynamic_update_slice.20
  875.6 12.5 fusion.177
  888.0 12.2 fusion.178
  909.3 19.7 dynamic_update_slice.20
  941.6 18.6 reduce-scatter.3.cloned.1.call-done
  966.3 28.5 %reduce-scatter.5.cloned.1.call-done = f32[1,1024,256]{1,2,0:T(8,128)} async-done(((f32[1,2048,256]{1,2,0:T(8,128)}), f32[1,1024,256]{1,2,0:T(8,128)}) %reduce-scatter.5.cloned.1.call-update) | async-done | bytes 1048592 | tf_op jit(solution)/shard_map/reduce_scatter | solution.py:244
  994.7 10.8 add_add_fusion
  1005.6 10.9 convolution_convert_fusion
  1016.5 12.1 fusion.114
  1038.3 11.9 fusion.80
  1065.5 231.1 %all-reduce.14.cloned.1.call-done = f32[1024,2048]{1,0:T(8,128)} async-done(((f32[1024,2048]{1,0:T(8,128)}), f32[1024,2048]{1,0:T(8,128)}) %all-reduce.14.cloned.1.call-update) | async-done | bytes 8388624 | tf_op jit(solution)/shard_map/psum | solution.py:260
  1302.6 26.4 %all-reduce = (f32[2048]{0:T(1024)}, f32[2048]{0:T(1024)}) all-reduce(f32[2048]{0:T(1024)S(1)} %get-tuple-element.213, f32[2048]{0:T(1024)S(1)} %copy-done.42), channel_id=1, replica_groups=mesh['dp'=4,'ctx'=2,'tensor'=4] {'dp','ctx'}, use_global_device_ids=true, to_apply=%region_19.20 | all-reduce | flops 4096 | bytes 32768 | tf_op jit(solution)/shard_map/psum | solution.py:278
  1329.0 124.5 %all-reduce.10.cloned.1.call-done = bf16[1024,2048]{1,0:T(8,128)(2,1)} async-done(((bf16[1024,2048]{1,0:T(8,128)(2,1)}), bf16[1024,2048]{1,0:T(8,128)(2,1)}) %all-reduce.10.cloned.1.call-update) | async-done | bytes 4194320 | tf_op jit(solution)/shard_map/psum | solution.py:216
  1453.5 19.9 fusion.57
  1473.4 536.6 %all-reduce.16.cloned.1.call-done = (f32[2048,512]{1,0:T(8,128)}, f32[2048,256]{1,0:T(8,128)}, f32[2048,256]{1,0:T(8,128)}, f32[512,2048]{1,0:T(8,128)}, f32[204...) async-done(((f32[2048,512]{1,0:T(8,128)}, f32[2048,256]{1,0:T(8,128)}, f32[2048,256]{1,0:T(8,128)}, f32[512,2048]{1,0:T(8,128)}, f32[2048,1408]{1,0:T(8,128)}, ...) | async-done | bytes 47185936 | tf_op jit(solution)/shard_map/psum | solution.py:278
  (239 shorter events, 294.0 us)
Async XLA Ops:
  7.2 99.5 %copy-start = (bf16[512,2048]{1,0:T(8,128)(2,1)S(1)}, bf16[512,2048]{1,0:T(8,128)(2,1)}, u32[]{:S(2)}) copy-start(bf16[512,2048]{1,0:T(8,128)(2,1)} %param.30) | copy-start | bytes 6291460
  7.2 38.1 %all-gather.4.cloned.1.call-start = ((), (), s32[]{:S(2)}) async-start(), calls=%async_computation.2 | async-start | bytes 1572864 | tf_op jit(solution)/shard_map/all_gather | solution.py:178
  14.5 19.7 copy-start.17
  14.5 19.7 copy-start.19
  19.6 47.6 %all-gather.6.cloned.1.call-start = ((), (), s32[]{:S(2)}) async-start(), calls=%async_computation.9 | async-start | bytes 1572864 | tf_op jit(solution)/shard_map/all_gather | solution.py:179
  24.3 380.4 %all-reduce.8.cloned.1.call-start = ((), (), s32[]{:S(2)}) async-start(), calls=%async_computation.3 | async-start | bytes 16777216 | tf_op jit(solution)/shard_map/psum | solution.py:196
  113.7 296.9 %copy-start.34 = (f32[2048]{0:T(1024)S(1)}, f32[2048]{0:T(1024)}, u32[]{:S(2)}) copy-start(f32[2048]{0:T(1024)} %param.26) | copy-start | bytes 24580
  113.7 644.4 %all-reduce.12.cloned.1.call-start = ((), (), s32[]{:S(2)}) async-start(), calls=%async_computation.5 | async-start | bytes 16777216 | tf_op jit(solution)/shard_map/psum | solution.py:218
  412.9 355.3 %copy-start.36 = (f32[1024]{0:T(1024)}, f32[1024]{0:T(1024)S(1)}, u32[]{:S(2)}) copy-start(f32[1024]{0:T(1024)S(1)} %add_rsqrt_fusion) | copy-start | bytes 12292
  468.1 492.0 %reduce-scatter.3.cloned.1.call-start = ((), (), s32[]{:S(2)}) async-start(), calls=%async_computation.6 | async-start | bytes 3145728 | tf_op jit(solution)/shard_map/reduce_scatter | solution.py:243
  832.6 23.5 %copy-start.4 = (f32[2048,2,128]{0,2,1:T(8,128)}, f32[2048,2,128]{0,2,1:T(8,128)S(1)}, u32[]{:S(2)}) copy-start(f32[2048,2,128]{0,2,1:T(8,128)S(1)} %fusion.179) | copy-start | bytes 6291460 | tf_op jit(solution)/shard_map/while
  905.5 23.5 %copy-start.4 = (f32[2048,2,128]{0,2,1:T(8,128)}, f32[2048,2,128]{0,2,1:T(8,128)S(1)}, u32[]{:S(2)}) copy-start(f32[2048,2,128]{0,2,1:T(8,128)S(1)} %fusion.179) | copy-start | bytes 6291460 | tf_op jit(solution)/shard_map/while
  929.1 65.6 %reduce-scatter.5.cloned.1.call-start = ((), (), s32[]{:S(2)}) async-start(), calls=%async_computation.7 | async-start | bytes 3145728 | tf_op jit(solution)/shard_map/reduce_scatter | solution.py:244
  929.7 366.8 %all-reduce.14.cloned.1.call-start = ((), (), s32[]{:S(2)}) async-start(), calls=%async_computation.8 | async-start | bytes 16777216 | tf_op jit(solution)/shard_map/psum | solution.py:260
  933.2 28.4 %copy-start.22 = (bf16[2048,256]{1,0:T(8,128)(2,1)S(1)}, bf16[2048,256]{1,0:T(8,128)(2,1)}, u32[]{:S(2)}) copy-start(bf16[2048,256]{1,0:T(8,128)(2,1)} %param.28) | copy-start | bytes 3145732
  933.3 28.2 %copy-start.28 = (bf16[1024,4,128]{0,2,1:T(8,128)(2,1)}, bf16[1024,4,128]{0,2,1:T(8,128)(2,1)S(1)}, u32[]{:S(2)}) copy-start(bf16[1024,4,128]{0,2,1:T(8,128)(2,1)S(1)} %maximum_convert_fusion) | copy-start | bytes 3145732
  961.5 33.2 %copy-start.32 = (bf16[2048,256]{1,0:T(8,128)(2,1)S(1)}, bf16[2048,256]{1,0:T(8,128)(2,1)}, u32[]{:S(2)}) copy-start(bf16[2048,256]{1,0:T(8,128)(2,1)} %param.29) | copy-start | bytes 3145732
  1005.5 448.0 %all-reduce.10.cloned.1.call-start = ((), (), s32[]{:S(2)}) async-start(), calls=%async_computation.4 | async-start | bytes 8388608 | tf_op jit(solution)/shard_map/psum | solution.py:216
  1038.2 971.7 %all-reduce.16.cloned.1.call-start = ((), (), s32[]{:S(2)}) async-start(), calls=%async_computation.10 | async-start | bytes 94371840 | tf_op jit(solution)/shard_map/psum | solution.py:278
  1065.4 237.2 %copy-start.42 = (f32[2048]{0:T(1024)S(1)}, f32[2048]{0:T(1024)}, u32[]{:S(2)}) copy-start(f32[2048]{0:T(1024)} %get-tuple-element.211) | copy-start | bytes 24580
  1065.5 388.1 %copy-start.35 = (f32[2048]{0:T(1024)S(1)}, f32[2048]{0:T(1024)}, u32[]{:S(2)}) copy-start(f32[2048]{0:T(1024)} %param.26) | copy-start | bytes 24580
  1065.5 388.0 %copy-start.37 = (f32[1024]{0:T(1024)S(1)}, f32[1024]{0:T(1024)}, u32[]{:S(2)}) copy-start(f32[1024]{0:T(1024)} %copy-done.36) | copy-start | bytes 12292
  1065.5 388.0 %copy-start.41 = (f32[1024]{0:T(1024)S(1)}, f32[1024]{0:T(1024)}, u32[]{:S(2)}) copy-start(f32[1024]{0:T(1024)} %copy-done.40) | copy-start | bytes 12292
  2029.0 20.2 copy-start.1
  (46 other events, 305.9 us)
Sparse Core Ops, SparseCore 0:
  19.8 23.9 all-gather.3
  45.9 21.2 all-gather.5
  113.8 290.8 all-reduce.7
  468.2 289.8 all-reduce.11
  929.3 30.8 reduce-scatter.2
  962.9 31.8 reduce-scatter.4
  1005.7 290.8 all-reduce.13
  1299.5 153.9 all-reduce.9
  1460.7 549.2 all-reduce.15
where the time goes:
time: 2060 us
  waiting for transfers between devices  1540 us (75%)
  matrix products  238 us (12%)
  local copies, waits for them, and re-layouts  136 us (7%)
  other arithmetic  98.8 us (5%)
  blocking collectives  26.4 us (1%)
    psum x1, waiting for transfers between devices, per_device(): lax.psum((grad_query, grad_key, grad_value, grad_output, grad_attn_gain,...  537 us
    psum x1, waiting for transfers between devices, per_device(): lax.psum(contract_cols(dgate, w_gate) + contract_cols(dupward, w_up), 'te...  290 us
    psum x1, waiting for transfers between devices, per_device(): attn_branch = lax.psum(attn_part, 'tensor')  288 us
    psum x1, waiting for transfers between devices, per_device(): lax.psum(contract_cols(dq_proj, w_query) + contract_cols(dk_proj, w_key)...  231 us
    psum x1, waiting for transfers between devices, per_device(): lax.psum(ffn_part.astype(jnp.bfloat16), 'tensor').astype(jnp.float32)  125 us
    dot_general x7, matrix products, contract_cols(): jnp.einsum('rc,dc->rd', left, right, preferred_element_type=jnp.float32)  63.1 us
    dot_general x7, matrix products, contract_rows(): jnp.einsum('rd,rf->df', left, right, preferred_element_type=jnp.float32)  48.8 us
    dynamic_update_slice x4, local copies, waits for them, and re-layouts, attend_back(): lax.scan(one_block, (empty, empty), (query_blocks, dmix_blocks, log_total...  46.9 us
  transfers between devices with their start and end apart: 9, of which 8 were waited for; matrix products, arithmetic and copies ran while one was open for 6% of the time, Pallas kernels for 0%

commit v1 on v0

v1 whole, which is shorter than its diff:
```python
import functools

import jax
import jax.numpy as jnp
from jax import lax
from jax.experimental import pallas as pl
from jax.experimental.pallas import tpu as pltpu
from jax.sharding import PartitionSpec as P

HEAD_DIM = 128
EPSILON = 1e-05
NEG_BIG = -1e30
FACTOR = HEAD_DIM ** (-0.5)
LOG2E = 1.4426950408889634
QUERY_BLOCK = 256
BF16 = jnp.bfloat16
F32 = jnp.float32

NT = (((1,), (1,)), ((), ()))


def nt_dot(left, right):
    return lax.dot_general(left, right, NT, preferred_element_type=F32)


def nn_dot(left, right):
    return jnp.dot(left, right, preferred_element_type=F32)


def stack_heads(block, group):
    return jnp.concatenate(
        [block[:, h * HEAD_DIM : (h + 1) * HEAD_DIM] for h in range(group)], axis=0
    )


def hide_later(scores, first_row, rows, fill):
    key_row = lax.broadcasted_iota(jnp.int32, scores.shape, 0)
    query_row = lax.broadcasted_iota(jnp.int32, scores.shape, 1) % rows + first_row
    return jnp.where(key_row <= query_row, scores, fill)


def attend_kernel(
    group, span, query_order, key_order, q_ref, k_ref, vt_ref, o_ref, lse_ref, top, total, acc
):
    rows = q_ref.shape[0]
    step = pl.program_id(1)
    first = step * rows
    order = query_order[first // span]
    queries = stack_heads(q_ref[...], group)
    top[...] = jnp.full_like(top, NEG_BIG)
    total[...] = jnp.zeros_like(total)
    acc[...] = jnp.zeros_like(acc)

    def visit(place, diagonal):
        keys = k_ref[pl.ds(place, span), :]
        scores = nt_dot(keys, queries) * (FACTOR * LOG2E)
        if diagonal:
            scores = hide_later(scores, first % span, rows, NEG_BIG)
        before = top[...]
        now = jnp.maximum(before, jnp.max(scores, axis=0, keepdims=True))
        weights = jnp.exp2(scores - now)
        shrink = jnp.exp2(before - now)
        top[...] = now
        total[...] = total[...] * shrink + jnp.sum(weights, axis=0, keepdims=True)
        acc[...] = acc[...] * shrink + nn_dot(
            vt_ref[:, pl.ds(place, span)], weights.astype(BF16)
        )

    def one_span(j, carry):
        place = pl.multiple_of(j * span, span)
        pl.when(key_order[j] < order)(lambda: visit(place, False))
        pl.when(key_order[j] == order)(lambda: visit(place, True))
        return carry

    lax.fori_loop(0, k_ref.shape[0] // span, one_span, 0)
    mixed = acc[...] / total[...]
    logs = top[...] + jnp.log2(total[...])
    for h in range(group):
        part = slice(h * rows, (h + 1) * rows)
        o_ref[:, h * HEAD_DIM : (h + 1) * HEAD_DIM] = mixed[:, part].T.astype(BF16)
        lse_ref[0, h : h + 1, :] = logs[:, part]


def attend(queries, keys, values, query_order, key_order, span):
    rows, width = queries.shape
    full, kv_width = keys.shape
    kv_heads = kv_width // HEAD_DIM
    group = width // kv_width
    block = min(QUERY_BLOCK, span)
    query_spec = pl.BlockSpec((block, group * HEAD_DIM), lambda g, i, *_: (i, g))
    return pl.pallas_call(
        functools.partial(attend_kernel, group, span),
        grid_spec=pltpu.PrefetchScalarGridSpec(
            num_scalar_prefetch=2,
            grid=(kv_heads, rows // block),
            in_specs=[
                query_spec,
                pl.BlockSpec((full, HEAD_DIM), lambda g, i, *_: (0, g)),
                pl.BlockSpec((HEAD_DIM, full), lambda g, i, *_: (g, 0)),
            ],
            out_specs=[
                query_spec,
                pl.BlockSpec((1, group, block), lambda g, i, *_: (g, 0, i)),
            ],
            scratch_shapes=[
                pltpu.VMEM((1, group * block), F32),
                pltpu.VMEM((1, group * block), F32),
                pltpu.VMEM((HEAD_DIM, group * block), F32),
            ],
        ),
        out_shape=[
            jax.ShapeDtypeStruct((rows, width), BF16),
            jax.ShapeDtypeStruct((kv_heads, group, rows), F32),
        ],
        compiler_params=pltpu.CompilerParams(vmem_limit_bytes=32 * 2**20),
        cost_estimate=pl.CostEstimate(
            flops=4 * rows * full * width,
            bytes_accessed=4 * rows * width + 4 * full * kv_width,
            transcendentals=rows * full * width // HEAD_DIM,
        ),
    )(query_order, key_order, queries, keys, values.T)


def attend_back_kernel(
    group,
    span,
    query_order,
    key_order,
    q_ref,
    do_ref,
    o_ref,
    lse_ref,
    cos_ref,
    sin_ref,
    k_ref,
    v_ref,
    kt_ref,
    dq_ref,
    dk_ref,
    dv_ref,
    acc,
):
    rows = q_ref.shape[0]
    step = pl.program_id(1)
    first = step * rows
    order = query_order[first // span]
    queries = stack_heads(q_ref[...], group)
    dmixed = stack_heads(do_ref[...], group)
    mixed = stack_heads(o_ref[...], group)
    product = dmixed.astype(F32) * mixed.astype(F32)
    delta = jnp.sum(product.T, axis=0, keepdims=True)
    logs = jnp.concatenate([lse_ref[0, h : h + 1, :] for h in range(group)], axis=1)
    acc[...] = jnp.zeros_like(acc)

    @pl.when(step == 0)
    def _():
        dk_ref[...] = jnp.zeros_like(dk_ref)
        dv_ref[...] = jnp.zeros_like(dv_ref)

    def visit(place, diagonal):
        here = pl.ds(place, span)
        scores = nt_dot(k_ref[here, :], queries) * (FACTOR * LOG2E)
        probs = jnp.exp2(scores - logs)
        if diagonal:
            probs = hide_later(probs, first % span, rows, 0.0)
        dprobs = nt_dot(v_ref[here, :], dmixed)
        dscore = (probs * (dprobs - delta)).astype(BF16)
        dv_ref[here, :] += nn_dot(probs.astype(BF16), dmixed)
        dk_ref[here, :] += nn_dot(dscore, queries)
        acc[...] += nn_dot(kt_ref[:, here], dscore)

    def one_span(j, carry):
        place = pl.multiple_of(j * span, span)
        pl.when(key_order[j] < order)(lambda: visit(place, False))
        pl.when(key_order[j] == order)(lambda: visit(place, True))
        return carry

    lax.fori_loop(0, k_ref.shape[0] // span, one_span, 0)
    half = HEAD_DIM // 2
    cosine, sine = cos_ref[...], sin_ref[...]
    for h in range(group):
        grad = acc[:, h * rows : (h + 1) * rows] * FACTOR
        leading, trailing = grad[:half], grad[half:]
        turned = jnp.concatenate(
            [leading * cosine + trailing * sine, trailing * cosine - leading * sine], axis=0
        )
        dq_ref[:, h * HEAD_DIM : (h + 1) * HEAD_DIM] = turned.T.astype(BF16)

    @pl.when(step == pl.num_programs(1) - 1)
    def _():
        dk_ref[...] = dk_ref[...] * FACTOR


def attend_back(
    queries, dmixed, mixed, logs, cosine, sine, keys, values, query_order, key_order, span
):
    rows, width = queries.shape
    full, kv_width = keys.shape
    kv_heads = kv_width // HEAD_DIM
    group = width // kv_width
    block = min(QUERY_BLOCK, span)
    half = HEAD_DIM // 2
    query_spec = pl.BlockSpec((block, group * HEAD_DIM), lambda g, i, *_: (i, g))
    key_spec = pl.BlockSpec((full, HEAD_DIM), lambda g, i, *_: (0, g))
    table_spec = pl.BlockSpec((half, block), lambda g, i, *_: (0, i))
    return pl.pallas_call(
        functools.partial(attend_back_kernel, group, span),
        grid_spec=pltpu.PrefetchScalarGridSpec(
            num_scalar_prefetch=2,
            grid=(kv_heads, rows // block),
            in_specs=[
                query_spec,
                query_spec,
                query_spec,
                pl.BlockSpec((1, group, block), lambda g, i, *_: (g, 0, i)),
                table_spec,
                table_spec,
                key_spec,
                key_spec,
                pl.BlockSpec((HEAD_DIM, full), lambda g, i, *_: (g, 0)),
            ],
            out_specs=[query_spec, key_spec, key_spec],
            scratch_shapes=[pltpu.VMEM((HEAD_DIM, group * block), F32)],
        ),
        out_shape=[
            jax.ShapeDtypeStruct((rows, width), BF16),
            jax.ShapeDtypeStruct((full, kv_width), F32),
            jax.ShapeDtypeStruct((full, kv_width), F32),
        ],
        compiler_params=pltpu.CompilerParams(vmem_limit_bytes=32 * 2**20),
        cost_estimate=pl.CostEstimate(
            flops=10 * rows * full * width,
            bytes_accessed=8 * rows * width + 14 * full * kv_width,
            transcendentals=rows * full * width // HEAD_DIM,
        ),
    )(
        query_order,
        key_order,
        queries,
        dmixed,
        mixed,
        logs,
        cosine.T,
        sine.T,
        keys,
        values,
        keys.T,
    )


def fold_steps(dp_size, ctx_size):
    steps = []
    bit = 1
    while bit < ctx_size:
        steps.append(("ctx", bit))
        bit *= 2
    along = []
    bit = 2
    while bit < dp_size:
        along.append(("dp", bit))
        bit *= 2
    even, odd = steps + along, along + steps
    plan = [((("dp", 1)), (("dp", 1)))] if dp_size > 1 else []
    return plan + list(zip(even, odd))


def step_perm(step, dp_size, ctx_size):
    pairs = []
    for d in range(dp_size):
        for c in range(ctx_size):
            axis, bit = step[d % 2]
            other = (d ^ bit, c) if axis == "dp" else (d, c ^ bit)
            pairs.append((d * ctx_size + c, other[0] * ctx_size + other[1]))
    return pairs


def step_bit(step):
    d, c = lax.axis_index("dp"), lax.axis_index("ctx")

    def of(axis, bit):
        return jnp.where(((d if axis == "dp" else c) & bit) != 0, 1, 0)

    return jnp.where(d % 2 == 0, of(*step[0]), of(*step[1]))


def sum_plane(grad, dp_size, ctx_size):
    plan = fold_steps(dp_size, ctx_size)
    pieces = grad
    perms = [step_perm(s, dp_size, ctx_size) for s in plan]
    bits = [step_bit(s) for s in plan]
    for perm, bit in zip(perms, bits):
        half = pieces.shape[0] // 2
        kept = lax.dynamic_slice_in_dim(pieces, bit * half, half, 0)
        sent = lax.dynamic_slice_in_dim(pieces, (1 - bit) * half, half, 0).astype(BF16)
        pieces = kept.astype(F32) + lax.ppermute(sent, ("dp", "ctx"), perm).astype(F32)
        if perm is not perms[-1]:
            pieces = pieces.astype(BF16)
    pieces = pieces.astype(BF16)
    for perm, bit in zip(perms[::-1], bits[::-1]):
        other = lax.ppermute(pieces, ("dp", "ctx"), perm)
        pieces = jnp.where(
            bit == 0,
            jnp.concatenate([pieces, other], 0),
            jnp.concatenate([other, pieces], 0),
        )
    return pieces.astype(F32)


def sequence_positions(order_row, length):
    spans = order_row.shape[0]
    stride = length // spans
    places = jnp.arange(length, dtype=jnp.int32)
    onehot = (places // stride)[:, None] == jnp.arange(spans, dtype=jnp.int32)[None, :]
    starts = jnp.sum(jnp.where(onehot, order_row[None, :], 0), axis=1)
    return starts * stride + places % stride


def rotary_tables(positions):
    inverse = 1.0 / 10000.0 ** (jnp.arange(0, HEAD_DIM, 2, dtype=F32) / HEAD_DIM)
    angle = positions.astype(F32)[:, None] * inverse[None, :]
    return (jnp.cos(angle), jnp.sin(angle))


def rotate(field, cosine, sine):
    half = field.shape[-1] // 2
    leading, trailing = (field[..., :half], field[..., half:])
    cosine, sine = (cosine[:, None, :], sine[:, None, :])
    return jnp.concatenate(
        [leading * cosine - trailing * sine, trailing * cosine + leading * sine], axis=-1
    )


def rotate_back(grad, cosine, sine):
    return rotate(grad, cosine, -sine)


def contract_rows(left, right):
    return jnp.einsum("rd,rf->df", left, right, preferred_element_type=F32)


def contract_cols(left, right):
    return jnp.einsum("rc,dc->rd", left, right, preferred_element_type=F32)


def norm_back(dnormed, unit, inverse, gain):
    scaled = dnormed * gain
    return inverse * (scaled - unit * jnp.mean(scaled * unit, axis=-1, keepdims=True))


def scatter_sum(part):
    return lax.psum_scatter(
        part.astype(BF16), "tensor", scatter_dimension=0, tiled=True
    ).astype(F32)


def gather_rows(part):
    return lax.all_gather(part.astype(BF16), "tensor", axis=0, tiled=True)


def swap_ctx(part, ctx_size):
    return [
        lax.ppermute(part, "ctx", [(i, (i + s) % ctx_size) for i in range(ctx_size)])
        for s in range(1, ctx_size)
    ]


def per_device(
    inputs,
    cotangent,
    skip_mask,
    group_ids,
    span_order,
    exit_scale,
    attn_gain,
    ffn_gain,
    w_query,
    w_key,
    w_value,
    w_output,
    w_gate,
    w_up,
    w_down,
):
    _, rows, width = inputs.shape
    dp_size, ctx_size, tensor_size = (lax.axis_size(a) for a in ("dp", "ctx", "tensor"))
    full_len = rows * ctx_size
    spans = span_order.shape[1]
    span = full_len // spans
    kv_local = w_key.shape[1] // HEAD_DIM
    ctx = lax.axis_index("ctx")
    offset = ctx * rows
    positions = lax.dynamic_slice_in_dim(sequence_positions(span_order[0], full_len), offset, rows)
    cosine, sine = rotary_tables(positions)
    keep = skip_mask[0].astype(F32)
    scale = jnp.where(group_ids[0] == 1, exit_scale[1], exit_scale[0])

    own_spans = spans // ctx_size
    orders = [
        lax.dynamic_slice_in_dim(span_order[0], ((ctx - s) % ctx_size) * own_spans, own_spans)
        for s in range(ctx_size)
    ]
    query_order, key_order = orders[0], jnp.concatenate(orders)

    x_low = inputs[0]
    flat = x_low.astype(F32)
    inv_one = lax.rsqrt(jnp.mean(flat * flat, axis=-1, keepdims=True) + EPSILON)
    normed_one = (flat * inv_one * attn_gain).astype(BF16)
    k_proj = nn_dot(normed_one, w_key).reshape(rows, kv_local, HEAD_DIM)
    keys_own = rotate(k_proj, cosine, sine).astype(BF16).reshape(rows, -1)
    values_own = nn_dot(normed_one, w_value).astype(BF16)
    keys = jnp.concatenate([keys_own] + swap_ctx(keys_own, ctx_size), 0)
    values = jnp.concatenate([values_own] + swap_ctx(values_own, ctx_size), 0)
    q_proj = nn_dot(normed_one, w_query).reshape(rows, -1, HEAD_DIM)
    queries = rotate(q_proj, cosine, sine).astype(BF16).reshape(rows, -1)
    mixed, logs = attend(queries, keys, values, query_order, key_order, span)

    own = rows // tensor_size
    first = lax.axis_index("tensor") * own
    take = lambda a: lax.dynamic_slice_in_dim(a, first, own, 0)
    x_own = take(x_low).astype(F32)
    dy_own = take(cotangent[0]).astype(F32) * scale
    attn_own = scatter_sum(nn_dot(mixed, w_output))
    hidden = x_own + attn_own
    inv_two = lax.rsqrt(jnp.mean(hidden * hidden, axis=-1, keepdims=True) + EPSILON)
    unit_two = hidden * inv_two
    normed_two = gather_rows(unit_two * ffn_gain)

    dscaled = cotangent[0].astype(F32) * scale
    dffn = (keep * dscaled).astype(BF16)
    dacted = contract_cols(dffn, w_down)
    gate = nn_dot(normed_two, w_gate)
    upward = nn_dot(normed_two, w_up)
    sigmoid_gate = jax.nn.sigmoid(gate)
    silu_gate = gate * sigmoid_gate
    acted = (silu_gate * upward).astype(BF16)
    dgate = (dacted * upward * sigmoid_gate * (1.0 + gate * (1.0 - sigmoid_gate))).astype(BF16)
    dupward = (dacted * silu_gate).astype(BF16)
    dnormed_own = scatter_sum(contract_cols(dgate, w_gate) + contract_cols(dupward, w_up))
    ffn_own = scatter_sum(nn_dot(acted, w_down))
    total = lambda g: sum_plane(g, dp_size, ctx_size)
    grad_down = total(contract_rows(acted, dffn))
    grad_gate = total(contract_rows(normed_two, dgate))
    grad_up = total(contract_rows(normed_two, dupward))
    grad_ffn_gain = jnp.sum(dnormed_own * unit_two, axis=0)
    dhidden = norm_back(dnormed_own, unit_two, inv_two, ffn_gain)
    dattn = gather_rows(keep * dy_own + dhidden)
    output = gather_rows(x_own + keep * (attn_own + ffn_own))
    grad_output = total(contract_rows(mixed, dattn))
    dmixed = contract_cols(dattn, w_output).astype(BF16)

    dq_proj, dkeys, dvalues = attend_back(
        queries, dmixed, mixed, logs, cosine, sine, keys, values, query_order, key_order, span
    )

    def collect(grad):
        parts = grad.reshape(ctx_size, rows, -1)
        summed = parts[0]
        for s in range(1, ctx_size):
            back = [(i, (i - s) % ctx_size) for i in range(ctx_size)]
            summed = summed + lax.ppermute(parts[s].astype(BF16), "ctx", back).astype(F32)
        return summed

    dk_own = collect(dkeys).reshape(rows, kv_local, HEAD_DIM)
    dk_proj = rotate_back(dk_own, cosine, sine).reshape(rows, -1).astype(BF16)
    dv_proj = collect(dvalues).astype(BF16)
    dnormed_one = scatter_sum(
        contract_cols(dq_proj, w_query)
        + contract_cols(dk_proj, w_key)
        + contract_cols(dv_proj, w_value)
    )
    grad_query = total(contract_rows(normed_one, dq_proj))
    grad_key = total(contract_rows(normed_one, dk_proj))
    grad_value = total(contract_rows(normed_one, dv_proj))
    inv_own = take(inv_one)
    unit_own = x_own * inv_own
    grad_attn_gain = jnp.sum(dnormed_one * unit_own, axis=0)
    grad_attn_gain, grad_ffn_gain = lax.psum(
        (grad_attn_gain, grad_ffn_gain), ("dp", "ctx", "tensor")
    )
    through = gather_rows(dhidden + norm_back(dnormed_one, unit_own, inv_own, attn_gain))
    input_grad = dscaled + through.astype(F32)
    return (
        output.reshape(inputs.shape),
        input_grad.reshape(inputs.shape),
        grad_attn_gain,
        grad_ffn_gain,
        grad_query,
        grad_key,
        grad_value,
        grad_output,
        grad_gate,
        grad_up,
        grad_down,
    )


def solution(mesh):
    rows = P("dp", "ctx", None)
    by_column, by_row = P(None, "tensor"), P("tensor", None)
    in_specs = (rows, rows, P("dp"), P("dp"), P("dp", None), P(), P(), P())
    in_specs += (by_column,) * 3 + (by_row,) + (by_column,) * 2 + (by_row,)
    out_specs = (rows, rows, P(), P()) + (by_column,) * 3 + (by_row,) + (by_column,) * 2 + (by_row,)
    return jax.shard_map(
        per_device, mesh=mesh, in_specs=in_specs, out_specs=out_specs, check_vma=False
    )
```

time: 2060 us -> 933 us (0.45)
  waiting for transfers between devices: 1540 us -> 448 us
  matrix products: 238 us -> 136 us
  local copies, waits for them, and re-layouts: 136 us -> 49.3 us
  Pallas kernels: 0 us -> 50.7 us
  starting transfers between devices: 0.58 us -> 50.8 us
  other arithmetic: 98.8 us -> 130 us
    psum x5 -> x0, waiting for transfers between devices: 1470 us -> none  [the longest x1 537 us: per_device(): lax.psum((grad_query, grad_key, grad_value, grad_output, grad_attn_gain,...]
    all_gather x2 -> x4, waiting for transfers between devices: 20.3 us -> 159 us  [gather_rows(): return lax.all_gather(part.astype(BF16), 'tensor', axis=0, tiled=True)]
    ppermute x0 -> x46, waiting for transfers between devices: none -> 138 us  [the longest x21 82.7 us: sum_plane(): lax.ppermute(sent, ('dp', 'ctx'), perm).astype(F32)]
    reduce_scatter x2 -> x4, waiting for transfers between devices: 47 us -> 151 us  [scatter_sum(): lax.psum_scatter(part.astype(BF16), 'tensor', scatter_dimension=0, tiled=...]
    dot_general x35 -> x21, matrix products: 238 us -> 136 us  [the longest x7 54.3 us: contract_cols(): return jnp.einsum('rc,dc->rd', left, right, preferred_element_type=F32)]
    pallas_call x0 -> x2, Pallas kernels: none -> 50.7 us  [the longest x1 28.7 us: attend_back(): pl.pallas_call(functools.partial(attend_back_kernel, group, span), grid_s...]
    ppermute x0 -> x46, starting transfers between devices: none -> 50 us  [the longest x21 24.1 us: sum_plane(): other = lax.ppermute(pieces, ('dp', 'ctx'), perm)]
    dynamic_update_slice x6 -> x0, local copies, waits for them, and re-layouts: 48 us -> none  [the longest x4 46.9 us: attend_back(): lax.scan(one_block, (empty, empty), (query_blocks, dmix_blocks, log_total...]
  transfers between devices with their start and end apart: 9 -> 54, of which waited for: 8 -> 26; matrix products, arithmetic and copies ran while one was open for 6% -> 20% of each run, Pallas kernels for 0% -> 0%
where the time goes in v1:
time: 933 us; the launch traced here: 925 us
  waiting for transfers between devices  448 us (48%)
  matrix products  136 us (15%)
  other arithmetic  130 us (14%)
  starting transfers between devices  50.8 us (5%)
  Pallas kernels  50.7 us (5%)
  local copies, waits for them, and re-layouts  49.3 us (5%)
  blocking collectives  42.6 us (5%)
  between operations  17.9 us (2%)
    all_gather x4, waiting for transfers between devices, gather_rows(): return lax.all_gather(part.astype(BF16), 'tensor', axis=0, tiled=True)  159 us
    reduce_scatter x4, waiting for transfers between devices, scatter_sum(): lax.psum_scatter(part.astype(BF16), 'tensor', scatter_dimension=0, tiled=...  151 us
    ppermute x21, waiting for transfers between devices, sum_plane(): lax.ppermute(sent, ('dp', 'ctx'), perm).astype(F32)  82.7 us
    dot_general x7, matrix products, contract_cols(): return jnp.einsum('rc,dc->rd', left, right, preferred_element_type=F32)  54.3 us
    ppermute x21, waiting for transfers between devices, sum_plane(): other = lax.ppermute(pieces, ('dp', 'ctx'), perm)  50.3 us
    dot_general x7, matrix products, nn_dot(): return jnp.dot(left, right, preferred_element_type=F32)  48.3 us
    psum x1, blocking collectives, per_device(): lax.psum((grad_attn_gain, grad_ffn_gain), ('dp', 'ctx', 'tensor'))  42.6 us
    convert_element_type x7, other arithmetic, sum_plane(): return pieces.astype(F32)  39.1 us
  transfers between devices with their start and end apart: 54, of which 26 were waited for; matrix products, arithmetic and copies ran while one was open for 20% of the time, Pallas kernels for 0%

profile of v1, /device:TPU:0, one launch (start us, length us, event | category | flops | bytes accessed | tf_op | source)
XLA Modules:
  0.0 925.0 jit_solution(2917818169591308565)
XLA Ops:
  52.5 22.1 %shard_map.230 = (bf16[1024,512]{1,0:T(8,128)(2,1)S(1)}, f32[2,2,1024]{2,1,0:T(2,128)S(1)}) custom-call(s32[2]{0:T(128)S(1)} %get-tuple-element.50.query_order, s32[4]{0:T(128)S(1)} %pad_add_fusion.key_order, bf16[1024,512]{1,0:T(8,128)(2,1)S(1)} %copy-done.6, bf16[2048,256]{1,0:T(8,128)(2,1)S(1)} %copy-done.8, bf16[256,2048]{1,0:T(8,128)(2,1)S(1)} %copy-done.10), custom_call_target="tpu_custom_call" | custom-call | flops 4294967296 | bytes 4194304 | tf_op jit(solution)/shard_map/pallas_call | solution.py:91
  79.5 75.7 %reduce-scatter.5.cloned.1.call-done = bf16[256,2048]{1,0:T(8,128)(2,1)} async-done(((bf16[1024,2048]{1,0:T(8,128)(2,1)}), bf16[256,2048]{1,0:T(8,128)(2,1)}) %reduce-scatter.5.cloned.1.call-update) | async-done | bytes 1048592 | tf_op jit(solution)/shard_map/reduce_scatter | solution.py:351
  163.4 78.2 %all-gather.5.cloned.1.call-done = bf16[1024,2048]{1,0:T(8,128)(2,1)} async-done(((bf16[256,2048]{1,0:T(8,128)(2,1)}), bf16[1024,2048]{1,0:T(8,128)(2,1)}) %all-gather.5.cloned.1.call-update) | async-done | bytes 4194320 | tf_op jit(solution)/shard_map/all_gather | solution.py:357
  241.6 11.8 %fusion.64 = f32[1024,1408]{1,0:T(8,128)} fusion(bf16[1024,2048]{1,0:T(8,128)(2,1)} %all-gather.5.cloned.1.call-done, bf16[2048,1408]{1,0:T(8,128)(2,1)} %param.28), kind=kOutput, calls=%fused_computation.181 | convolution fusion | flops 5905580032 | bytes 15728640 | tf_op jit(solution)/shard_map/dot_general | solution.py:27
  253.4 10.4 %fusion.63 = f32[1024,1408]{1,0:T(8,128)} fusion(bf16[1024,2048]{1,0:T(8,128)(2,1)S(1)} %copy-done.39, bf16[2048,1408]{1,0:T(8,128)(2,1)} %param.27), kind=kOutput, calls=%fused_computation.180 | convolution fusion | flops 5905580032 | bytes 15728640 | tf_op jit(solution)/shard_map/dot_general | solution.py:27
  263.8 15.3 %multiply_convert_fusion = (bf16[1024,1408]{1,0:T(8,128)(2,1)}, bf16[1024,1408]{1,0:T(8,128)(2,1)}, bf16[1024,1408]{1,0:T(8,128)(2,1)}) fusion(f32[1024,1408]{1,0:T(8,128)} %fusion.63, f32[1024,1408]{1,0:T(8,128)} %fusion.64, bf16[1408,2048]{1,0:T(8,128)(2,1)} %param.29, bf16[1,1024,2048]{2,1,0:T(8,128)(2,1)S(1)} %copy-done.19, f32[]{:T(128)} %bitcast.1, ...), kind=kOutput, calls=%fused_computation.28 | convolution fusion | flops 5935595520 | bytes 30146568 | tf_op jit(solution)/shard_map/rc,dc->rd/dot_general | solution.py:342
  279.1 9.7 %fusion.65 = f32[1024,2048]{1,0:T(8,128)S(1)} fusion(bf16[1024,1408]{1,0:T(8,128)(2,1)} %get-tuple-element.28, bf16[2048,1408]{1,0:T(8,128)(2,1)} %param.27), kind=kOutput, calls=%fused_computation.182 | convolution fusion | flops 5905580032 | bytes 17039360 | tf_op jit(solution)/shard_map/rc,dc->rd/dot_general | solution.py:342
  288.9 11.0 %add_convert_fusion.1 = bf16[1024,2048]{1,0:T(8,128)(2,1)} fusion(f32[1024,2048]{1,0:T(8,128)S(1)} %fusion.65, bf16[1024,1408]{1,0:T(8,128)(2,1)S(1)} %copy-done.43, bf16[2048,1408]{1,0:T(8,128)(2,1)} %param.28), kind=kOutput, calls=%fused_computation.14 | convolution fusion | flops 5909774336 | bytes 21233664 | tf_op jit(solution)/shard_map/rc,dc->rd/dot_general | solution.py:342
  299.9 75.4 %reduce-scatter.9.cloned.1.call-done = bf16[256,2048]{1,0:T(8,128)(2,1)} async-done(((bf16[1024,2048]{1,0:T(8,128)(2,1)}), bf16[256,2048]{1,0:T(8,128)(2,1)}) %reduce-scatter.9.cloned.1.call-update) | async-done | bytes 1048592 | tf_op jit(solution)/shard_map/reduce_scatter | solution.py:351
  384.6 79.4 %all-gather.9.cloned.1.call-done = bf16[1024,2048]{1,0:T(8,128)(2,1)} async-done(((bf16[256,2048]{1,0:T(8,128)(2,1)}), bf16[1024,2048]{1,0:T(8,128)(2,1)}) %all-gather.9.cloned.1.call-update) | async-done | bytes 4194320 | tf_op jit(solution)/shard_map/all_gather | solution.py:357
  468.7 28.7 %shard_map.231 = (bf16[1024,512]{1,0:T(8,128)(2,1)S(1)}, f32[2048,256]{1,0:T(8,128)S(1)}, f32[2048,256]{1,0:T(8,128)S(1)}) custom-call(s32[2]{0:T(128)S(1)} %get-tuple-element.50.query_order, s32[4]{0:T(128)S(1)} %pad_add_fusion.key_order, bf16[1024,512]{1,0:T(8,128)(2,1)S(1)} %copy-done.7, bf16[1024,512]{1,0:T(8,128)(2,1)S(1)} %convolution_convert_fusion.2.do_ref, ...), custom_call_target="tpu_custom_call" | custom-call | flops 10737418240 | bytes 11534336 | tf_op jit(solution)/shard_map/pallas_call | solution.py:206
  526.8 9.6 %fusion.19 = f32[1408,2048]{1,0:T(8,128)S(1)} fusion(bf16[1024,1408]{1,0:T(8,128)(2,1)} %get-tuple-element.29, bf16[1,1024,2048]{2,1,0:T(8,128)(2,1)} %param.16, f32[]{:T(128)} %bitcast.1, f32[]{:T(128)} %bitcast.17), kind=kOutput, calls=%fused_computation.41 | convolution fusion | flops 5913968640 | bytes 18612232 | tf_op jit(solution)/shard_map/rd,rf->df/dot_general | solution.py:338
  570.5 8.2 convolution_convert_fusion
  606.6 20.7 %collective-permute-done.35 = bf16[512,1408]{1,0:T(8,128)(2,1)S(1)} collective-permute-done((bf16[512,1408]{1,0:T(8,128)(2,1)}, bf16[512,1408]{1,0:T(8,128)(2,1)S(1)}, u32[]{:S(2)}, u32[]{:S(2)}) %collective-permute-start.35) | collective-permute-done | bytes 1441824 | tf_op jit(solution)/shard_map/ppermute | solution.py:295
  629.6 20.8 %collective-permute-done.29 = bf16[512,1408]{1,0:T(8,128)(2,1)S(1)} collective-permute-done((bf16[512,1408]{1,0:T(8,128)(2,1)S(1)}, bf16[512,1408]{1,0:T(8,128)(2,1)S(1)}, u32[]{:S(2)}, u32[]{:S(2)}) %collective-permute-start.29) | collective-permute-done | bytes 1441824 | tf_op jit(solution)/shard_map/ppermute | solution.py:295
  665.4 8.8 collective-permute-done.30
  677.2 12.6 %collective-permute-done.37 = bf16[256,1408]{1,0:T(8,128)(2,1)} collective-permute-done((bf16[256,1408]{1,0:T(8,128)(2,1)}, bf16[256,1408]{1,0:T(8,128)(2,1)}, u32[]{:S(2)}, u32[]{:S(2)}) %collective-permute-start.37) | collective-permute-done | bytes 720928 | tf_op jit(solution)/shard_map/ppermute | solution.py:300
  695.1 10.1 %collective-permute-done.31 = bf16[256,1408]{1,0:T(8,128)(2,1)} collective-permute-done((bf16[256,1408]{1,0:T(8,128)(2,1)}, bf16[256,1408]{1,0:T(8,128)(2,1)}, u32[]{:S(2)}, u32[]{:S(2)}) %collective-permute-start.31) | collective-permute-done | bytes 720928 | tf_op jit(solution)/shard_map/ppermute | solution.py:300
  721.6 9.2 collective-permute-done.32
  745.0 10.0 %fusion.11 = f32[1408,2048]{1,0:T(8,128)} fusion(bf16[704,2048]{1,0:T(8,128)(2,1)} %collective-permute-done.45, bf16[704,2048]{1,0:T(8,128)(2,1)} %maximum_select_fusion.5, pred[]{:T(512)S(6)} %eq.47), kind=kLoop, calls=%fused_computation.21 | loop fusion | flops 28835840 | bytes 17301504 | tf_op jit(solution)/shard_map/convert_element_type | solution.py:306
  830.6 10.3 %fusion.9 = f32[2048,1408]{1,0:T(8,128)} fusion(bf16[1024,1408]{1,0:T(8,128)(2,1)} %collective-permute-done.33, bf16[1024,1408]{1,0:T(8,128)(2,1)} %maximum_select_fusion.3, pred[]{:T(512)S(6)} %eq.47), kind=kLoop, calls=%fused_computation.17 | loop fusion | flops 28835840 | bytes 17301504 | tf_op jit(solution)/shard_map/convert_element_type | solution.py:306
  843.4 10.2 %fusion.10 = f32[2048,1408]{1,0:T(8,128)} fusion(bf16[1024,1408]{1,0:T(8,128)(2,1)} %collective-permute-done.39, bf16[1024,1408]{1,0:T(8,128)(2,1)} %maximum_select_fusion.4, pred[]{:T(512)S(6)} %eq.47), kind=kLoop, calls=%fused_computation.19 | loop fusion | flops 28835840 | bytes 17301504 | tf_op jit(solution)/shard_map/convert_element_type | solution.py:306
  862.2 42.6 %all-reduce = (f32[2048]{0:T(1024)}, f32[2048]{0:T(1024)}) all-reduce(f32[2048]{0:T(1024)S(1)} %get-tuple-element.23, f32[2048]{0:T(1024)S(1)} %copy-done.34), channel_id=1, replica_groups=mesh['dp'=4,'ctx'=2,'tensor'=4] {'dp','ctx','tensor'}, use_global_device_ids=true, to_apply=%region_10.11 | all-reduce | flops 4096 | bytes 32768 | tf_op jit(solution)/shard_map/psum | solution.py:477
  905.9 9.0 fusion.8
  (328 shorter events, 307.3 us)
Async XLA Ops:
  7.2 148.0 %reduce-scatter.5.cloned.1.call-start = ((), (), s32[]{:S(2)}) async-start(), calls=%async_computation.4 | async-start | bytes 5242880 | tf_op jit(solution)/shard_map/reduce_scatter | solution.py:351
  14.2 30.9 %collective-permute-start.1 = (bf16[1024,256]{1,0:T(8,128)(2,1)}, bf16[1024,256]{1,0:T(8,128)(2,1)}, u32[]{:S(2)}, u32[]{:S(2)}) collective-permute-start(bf16[1024,256]{1,0:T(8,128)(2,1)} %convolution_convert_fusion.3), channel_id=1, source_target_pairs={{0,4},{4,0},{1,5},{5,1},{2,6},{6,2},{3,7},{7,3},{8,12},{12,8},{9,1... | collective-permute-start | bytes 1572872 | tf_op jit(solution)/shard_map/ppermute | solution.py:362
  79.0 162.6 %all-gather.5.cloned.1.call-start = ((), (), s32[]{:S(2)}) async-start(), calls=%async_computation.5 | async-start | bytes 5242880 | tf_op jit(solution)/shard_map/all_gather | solution.py:357
  160.1 215.2 %reduce-scatter.9.cloned.1.call-start = ((), (), s32[]{:S(2)}) async-start(), calls=%async_computation.8 | async-start | bytes 5242880 | tf_op jit(solution)/shard_map/reduce_scatter | solution.py:351
  299.9 164.1 %all-gather.9.cloned.1.call-start = ((), (), s32[]{:S(2)}) async-start(), calls=%async_computation.9 | async-start | bytes 5242880 | tf_op jit(solution)/shard_map/all_gather | solution.py:357
  382.6 354.5 %reduce-scatter.11.cloned.1.call-start = ((), (), s32[]{:S(2)}) async-start(), calls=%async_computation.10 | async-start | bytes 5242880 | tf_op jit(solution)/shard_map/reduce_scatter | solution.py:351
  526.7 212.7 %reduce-scatter.7.cloned.1.call-start = ((), (), s32[]{:S(2)}) async-start(), calls=%async_computation.6 | async-start | bytes 5242880 | tf_op jit(solution)/shard_map/reduce_scatter | solution.py:351
  542.6 36.1 %collective-permute-start.40 = (bf16[704,2048]{1,0:T(8,128)(2,1)}, bf16[704,2048]{1,0:T(8,128)(2,1)}, u32[]{:S(2)}, u32[]{:S(2)}) collective-permute-start(bf16[704,2048]{1,0:T(8,128)(2,1)} %dynamic-slice_convert_fusion), channel_id=1, source_target_pairs={{0,8},{4,12},{8,0},{12,4},{16,24},{20,28},{24,16},{28,20},{1,9},{5... | collective-permute-start | bytes 8650760 | tf_op jit(solution)/shard_map/ppermute | solution.py:295
  555.7 30.6 %collective-permute-start.34 = (bf16[1024,1408]{1,0:T(8,128)(2,1)}, bf16[1024,1408]{1,0:T(8,128)(2,1)}, u32[]{:S(2)}, u32[]{:S(2)}) collective-permute-start(bf16[1024,1408]{1,0:T(8,128)(2,1)} %dynamic-slice_convert_fusion.1), channel_id=1, source_target_pairs={{0,8},{4,12},{8,0},{12,4},{16,24},{20,28},{24,16},{28,20},{1,9},{5... | collective-permute-start | bytes 8650760 | tf_op jit(solution)/shard_map/ppermute | solution.py:295
  569.5 22.9 %collective-permute-start.28 = (bf16[1024,1408]{1,0:T(8,128)(2,1)}, bf16[1024,1408]{1,0:T(8,128)(2,1)}, u32[]{:S(2)}, u32[]{:S(2)}) collective-permute-start(bf16[1024,1408]{1,0:T(8,128)(2,1)} %dynamic-slice_convert_fusion.2), channel_id=1, source_target_pairs={{0,8},{4,12},{8,0},{12,4},{16,24},{20,28},{24,16},{28,20},{1,9},{5... | collective-permute-start | bytes 8650760 | tf_op jit(solution)/shard_map/ppermute | solution.py:295
  578.7 326.1 %all-gather.7.cloned.1.call-start = ((), (), s32[]{:S(2)}) async-start(), calls=%async_computation.7 | async-start | bytes 5242880 | tf_op jit(solution)/shard_map/all_gather | solution.py:357
  591.6 35.6 %collective-permute-start.35 = (bf16[512,1408]{1,0:T(8,128)(2,1)}, bf16[512,1408]{1,0:T(8,128)(2,1)S(1)}, u32[]{:S(2)}, u32[]{:S(2)}) collective-permute-start(bf16[512,1408]{1,0:T(8,128)(2,1)} %constant_dynamic-slice_fusion.3), channel_id=1, source_target_pairs={{0,4},{4,0},{8,24},{12,28},{16,20},{20,16},{24,8},{28,12},{1,5},{5... | collective-permute-start | bytes 4325384 | tf_op jit(solution)/shard_map/ppermute | solution.py:295
  595.0 55.4 %collective-permute-start.29 = (bf16[512,1408]{1,0:T(8,128)(2,1)S(1)}, bf16[512,1408]{1,0:T(8,128)(2,1)S(1)}, u32[]{:S(2)}, u32[]{:S(2)}) collective-permute-start(bf16[512,1408]{1,0:T(8,128)(2,1)S(1)} %constant_dynamic-slice_fusion.5), channel_id=1, source_target_pairs={{0,4},{4,0},{8,24},{12,28},{16,20},{20,16},{24,8},{28,12},{1,5},{5... | collective-permute-start | bytes 4325384 | tf_op jit(solution)/shard_map/ppermute | solution.py:295
  604.6 46.1 %collective-permute-start.42 = (bf16[176,2048]{1,0:T(8,128)(2,1)S(1)}, bf16[176,2048]{1,0:T(8,128)(2,1)S(1)}, u32[]{:S(2)}, u32[]{:S(2)}) collective-permute-start(bf16[176,2048]{1,0:T(8,128)(2,1)S(1)} %constant_dynamic-slice_fusion), channel_id=1, source_target_pairs={{0,16},{4,20},{8,12},{12,8},{16,0},{20,4},{24,28},{28,24},{1,17},{... | collective-permute-start | bytes 2162696 | tf_op jit(solution)/shard_map/ppermute | solution.py:295
  627.6 25.6 %collective-permute-start.36 = (bf16[256,1408]{1,0:T(8,128)(2,1)S(1)}, bf16[256,1408]{1,0:T(8,128)(2,1)S(1)}, u32[]{:S(2)}, u32[]{:S(2)}) collective-permute-start(bf16[256,1408]{1,0:T(8,128)(2,1)S(1)} %constant_dynamic-slice_fusion.2), channel_id=1, source_target_pairs={{0,16},{4,20},{8,12},{12,8},{16,0},{20,4},{24,28},{28,24},{1,17},{... | collective-permute-start | bytes 2162696 | tf_op jit(solution)/shard_map/ppermute | solution.py:295
  654.3 35.5 %collective-permute-start.37 = (bf16[256,1408]{1,0:T(8,128)(2,1)}, bf16[256,1408]{1,0:T(8,128)(2,1)}, u32[]{:S(2)}, u32[]{:S(2)}) collective-permute-start(bf16[256,1408]{1,0:T(8,128)(2,1)} %add_convert_fusion.11), channel_id=1, source_target_pairs={{0,16},{4,20},{8,12},{12,8},{16,0},{20,4},{24,28},{28,24},{1,17},{... | collective-permute-start | bytes 2162696 | tf_op jit(solution)/shard_map/ppermute | solution.py:300
  663.9 46.6 %collective-permute-start.44 = (bf16[352,2048]{1,0:T(8,128)(2,1)}, bf16[352,2048]{1,0:T(8,128)(2,1)}, u32[]{:S(2)}, u32[]{:S(2)}) collective-permute-start(bf16[352,2048]{1,0:T(8,128)(2,1)} %maximum_select_fusion.10), channel_id=1, source_target_pairs={{0,4},{4,0},{8,24},{12,28},{16,20},{20,16},{24,8},{28,12},{1,5},{5... | collective-permute-start | bytes 4325384 | tf_op jit(solution)/shard_map/ppermute | solution.py:300
  675.2 30.0 %collective-permute-start.31 = (bf16[256,1408]{1,0:T(8,128)(2,1)}, bf16[256,1408]{1,0:T(8,128)(2,1)}, u32[]{:S(2)}, u32[]{:S(2)}) collective-permute-start(bf16[256,1408]{1,0:T(8,128)(2,1)} %add_convert_fusion.12), channel_id=1, source_target_pairs={{0,16},{4,20},{8,12},{12,8},{16,0},{20,4},{24,28},{28,24},{1,17},{... | collective-permute-start | bytes 2162696 | tf_op jit(solution)/shard_map/ppermute | solution.py:300
  715.2 29.8 %collective-permute-start.45 = (bf16[704,2048]{1,0:T(8,128)(2,1)}, bf16[704,2048]{1,0:T(8,128)(2,1)}, u32[]{:S(2)}, u32[]{:S(2)}) collective-permute-start(bf16[704,2048]{1,0:T(8,128)(2,1)} %maximum_select_fusion.5), channel_id=1, source_target_pairs={{0,8},{4,12},{8,0},{12,4},{16,24},{20,28},{24,16},{28,20},{1,9},{5... | collective-permute-start | bytes 8650760 | tf_op jit(solution)/shard_map/ppermute | solution.py:300
  720.4 123.0 %collective-permute-start.39 = (bf16[1024,1408]{1,0:T(8,128)(2,1)}, bf16[1024,1408]{1,0:T(8,128)(2,1)}, u32[]{:S(2)}, u32[]{:S(2)}) collective-permute-start(bf16[1024,1408]{1,0:T(8,128)(2,1)} %maximum_select_fusion.4), channel_id=1, source_target_pairs={{0,8},{4,12},{8,0},{12,4},{16,24},{20,28},{24,16},{28,20},{1,9},{5... | collective-permute-start | bytes 8650760 | tf_op jit(solution)/shard_map/ppermute | solution.py:300
  736.1 94.1 %collective-permute-start.33 = (bf16[1024,1408]{1,0:T(8,128)(2,1)}, bf16[1024,1408]{1,0:T(8,128)(2,1)}, u32[]{:S(2)}, u32[]{:S(2)}) collective-permute-start(bf16[1024,1408]{1,0:T(8,128)(2,1)} %maximum_select_fusion.3), channel_id=1, source_target_pairs={{0,8},{4,12},{8,0},{12,4},{16,24},{20,28},{24,16},{28,20},{1,9},{5... | collective-permute-start | bytes 8650760 | tf_op jit(solution)/shard_map/ppermute | solution.py:300
  744.9 161.0 %all-gather.11.cloned.1.call-start = ((), (), s32[]{:S(2)}) async-start(), calls=%async_computation.11 | async-start | bytes 5242880 | tf_op jit(solution)/shard_map/all_gather | solution.py:357
  768.0 33.2 %collective-permute-start.23 = (bf16[128,2048]{1,0:T(8,128)(2,1)}, bf16[128,2048]{1,0:T(8,128)(2,1)}, u32[]{:S(2)}, u32[]{:S(2)}) collective-permute-start(bf16[128,2048]{1,0:T(8,128)(2,1)} %constant_dynamic-slice_fusion.7), channel_id=1, source_target_pairs={{0,4},{4,0},{8,24},{12,28},{16,20},{20,16},{24,8},{28,12},{1,5},{5... | collective-permute-start | bytes 1572872 | tf_op jit(solution)/shard_map/ppermute | solution.py:295
  801.2 39.7 %collective-permute-start.14 = (bf16[512,256]{1,0:T(8,128)(2,1)S(1)}, bf16[512,256]{1,0:T(8,128)(2,1)S(1)}, u32[]{:S(2)}, u32[]{:S(2)}) collective-permute-start(bf16[512,256]{1,0:T(8,128)(2,1)S(1)} %maximum_select_fusion.19), channel_id=1, source_target_pairs={{0,4},{4,0},{8,24},{12,28},{16,20},{20,16},{24,8},{28,12},{1,5},{5... | collective-permute-start | bytes 786440 | tf_op jit(solution)/shard_map/ppermute | solution.py:300
  (82 other events, 942.0 us)
Sparse Core Ops, SparseCore 0:
  79.1 76.1 reduce-scatter.4
  160.3 81.2 all-gather.4
  300.0 75.2 reduce-scatter.8
  382.7 81.2 all-gather.8
  526.9 74.9 reduce-scatter.10
  604.7 77.2 reduce-scatter.6
  745.0 78.9 all-gather.6
  825.6 80.2 all-gather.10

commit v2 on v1

--- a/solution.py
+++ b/solution.py
@@ -306,6 +306,184 @@
     return pieces.astype(F32)
 
 
+LINE_CHUNK = 32
+
+
+def line_kernel(size, chunk, streams, owners, side_count, out_count, *refs):
+    parts, refs = refs[:streams], refs[streams:]
+    sides, refs = refs[:side_count], refs[side_count:]
+    shared, refs = refs[:streams], refs[streams:]
+    kept, refs = refs[:out_count], refs[out_count:]
+    inbox, send_up, recv_up, send_back, recv_back = refs
+    half = parts[0].shape[0] // 2
+    count = half // chunk
+    last = size - 1
+    me = lax.axis_index("tensor")
+    above, below = jnp.minimum(me + 1, last), jnp.maximum(me - 1, 0)
+    flows = ((me, above, below), (last - me, below, above))
+
+    barrier = pltpu.get_barrier_semaphore()
+
+    def greet(other):
+        pl.semaphore_signal(
+            barrier, inc=1, device_id={"tensor": other}, device_id_type=pl.DeviceIdType.MESH
+        )
+
+    pl.when(me < last)(lambda: greet(above))
+    pl.when(me > 0)(lambda: greet(below))
+    pl.semaphore_wait(barrier, jnp.where((me > 0) & (me < last), 2, 1))
+
+    def place(f, i):
+        return pl.ds(pl.multiple_of(f * half + i * chunk, chunk), chunk)
+
+    def local(i):
+        return pl.ds(pl.multiple_of(i * chunk, chunk), chunk)
+
+    def onward(k, f, i, source):
+        return pltpu.make_async_remote_copy(
+            src_ref=source,
+            dst_ref=inbox.at[k, f, local(i)],
+            send_sem=send_up.at[k, f, i],
+            recv_sem=recv_up.at[k, f, i],
+            device_id={"tensor": flows[f][1]},
+            device_id_type=pl.DeviceIdType.MESH,
+        )
+
+    def backward(k, f, i):
+        block = shared[k].at[place(f, i)]
+        return pltpu.make_async_remote_copy(
+            src_ref=block,
+            dst_ref=block,
+            send_sem=send_back.at[k, f, i],
+            recv_sem=recv_back.at[k, f, i],
+            device_id={"tensor": flows[f][2]},
+            device_id_type=pl.DeviceIdType.MESH,
+        )
+
+    def reduce_chunk(k, f, i):
+        position = flows[f][0]
+        mine = parts[k].at[place(f, i)]
+        slot = inbox.at[k, f, local(i)]
+
+        @pl.when(position == 0)
+        def _():
+            onward(k, f, i, mine).start()
+
+        @pl.when(position > 0)
+        def _():
+            onward(k, f, i, slot).wait_recv()
+            total = slot[...].astype(F32) + mine[...].astype(F32)
+
+            @pl.when(position < last)
+            def _():
+                slot[...] = total.astype(BF16)
+                onward(k, f, i, slot).start()
+
+            @pl.when(position == last)
+            def _():
+                result = owners[k](total, place(f, i), local(i), sides, kept)
+                shared[k][place(f, i), :] = result.astype(BF16)
+                backward(k, f, i).start()
+
+    def pass_back(k, f, i):
+        position = flows[f][0]
+
+        @pl.when((position < last) & (i >= 0) & (i < count))
+        def _():
+            backward(k, f, i).wait_recv()
+            pl.when(position > 0)(lambda: backward(k, f, i).start())
+
+    def step(s, carry):
+        @pl.when(s < count)
+        def _():
+            for k in range(streams):
+                for f in range(2):
+                    reduce_chunk(k, f, s)
+
+        for k in range(streams):
+            for f in range(2):
+                pass_back(k, f, s - 2 * (last - flows[f][0]))
+        return carry
+
+    for ref in kept:
+        if ref.shape[0] == 1:
+            ref[...] = jnp.zeros_like(ref)
+    lax.fori_loop(0, count + 2 * last, step, 0)
+
+    def drain(i, carry):
+        for k in range(streams):
+            for f in range(2):
+                position = flows[f][0]
+                pl.when(position < last)(
+                    lambda: onward(k, f, i, inbox.at[k, f, local(i)]).wait_send()
+                )
+                pl.when(position > 0)(lambda: backward(k, f, i).wait_send())
+        return carry
+
+    lax.fori_loop(0, count, drain, 0)
+
+
+def line_sum(parts, owners, sides, kept, collective_id):
+    rows, width = parts[0].shape
+    size = lax.axis_size("tensor")
+    streams = len(parts)
+    chunk = min(LINE_CHUNK, rows // 2)
+    count = rows // 2 // chunk
+    whole = pl.BlockSpec(memory_space=pltpu.VMEM)
+    scalar = pl.BlockSpec(memory_space=pltpu.SMEM)
+    sems = pltpu.SemaphoreType.DMA((streams, 2, count))
+    outs = [jax.ShapeDtypeStruct((rows, width), BF16)] * streams + list(kept)
+    return pl.pallas_call(
+        functools.partial(line_kernel, size, chunk, streams, owners, len(sides), len(kept)),
+        out_shape=outs,
+        in_specs=[whole] * streams + [scalar if s.ndim == 1 else whole for s in sides],
+        out_specs=[whole] * len(outs),
+        scratch_shapes=[pltpu.VMEM((streams, 2, rows // 2, width), BF16)] + [sems] * 4,
+        compiler_params=pltpu.CompilerParams(
+            collective_id=collective_id, has_side_effects=True, vmem_limit_bytes=56 * 2**20
+        ),
+        cost_estimate=pl.CostEstimate(
+            flops=streams * rows * width,
+            bytes_accessed=streams * 300 * 2**20,
+            transcendentals=0,
+        ),
+    )(*parts, *sides)
+
+
+def unit_of(rows):
+    inverse = lax.rsqrt(jnp.mean(rows * rows, axis=-1, keepdims=True) + EPSILON)
+    return rows * inverse, inverse
+
+
+def own_hidden(total, where, here, sides, kept):
+    x_ref, gain_ref = sides
+    hidden = x_ref[where, :].astype(F32) + total
+    kept[0][here, :] = hidden
+    return unit_of(hidden)[0] * gain_ref[...]
+
+
+def own_dhidden(total, where, here, sides, kept):
+    hidden_ref, cot_ref, gain_ref, factor = sides
+    unit, inverse = unit_of(hidden_ref[here, :])
+    kept[1][...] += jnp.sum(total * unit, axis=0, keepdims=True)
+    dhidden = norm_back(total, unit, inverse, gain_ref[...])
+    kept[0][here, :] = dhidden
+    return cot_ref[where, :].astype(F32) * factor[0] + dhidden
+
+
+def own_dinput(total, where, here, sides, kept):
+    x_ref, hidden_ref, dhidden_ref, gain_ref, factor = sides
+    unit, inverse = unit_of(x_ref[where, :].astype(F32))
+    kept[0][...] += jnp.sum(total * unit, axis=0, keepdims=True)
+    return dhidden_ref[here, :] + norm_back(total, unit, inverse, gain_ref[...])
+
+
+def own_output(total, where, here, sides, kept):
+    x_ref, hidden_ref, dhidden_ref, gain_ref, factor = sides
+    x = x_ref[where, :].astype(F32)
+    return x + factor[0] * ((hidden_ref[here, :] - x) + total)
+
+
 def sequence_positions(order_row, length):
     spans = order_row.shape[0]
     stride = length // spans
@@ -345,16 +523,6 @@
 def norm_back(dnormed, unit, inverse, gain):
     scaled = dnormed * gain
     return inverse * (scaled - unit * jnp.mean(scaled * unit, axis=-1, keepdims=True))
-
-
-def scatter_sum(part):
-    return lax.psum_scatter(
-        part.astype(BF16), "tensor", scatter_dimension=0, tiled=True
-    ).astype(F32)
-
-
-def gather_rows(part):
-    return lax.all_gather(part.astype(BF16), "tensor", axis=0, tiled=True)
 
 
 def swap_ctx(part, ctx_size):
@@ -382,7 +550,7 @@
     w_down,
 ):
     _, rows, width = inputs.shape
-    dp_size, ctx_size, tensor_size = (lax.axis_size(a) for a in ("dp", "ctx", "tensor"))
+    dp_size, ctx_size = lax.axis_size("dp"), lax.axis_size("ctx")
     full_len = rows * ctx_size
     spans = span_order.shape[1]
     span = full_len // spans
@@ -414,16 +582,13 @@
     queries = rotate(q_proj, cosine, sine).astype(BF16).reshape(rows, -1)
     mixed, logs = attend(queries, keys, values, query_order, key_order, span)
 
-    own = rows // tensor_size
-    first = lax.axis_index("tensor") * own
-    take = lambda a: lax.dynamic_slice_in_dim(a, first, own, 0)
-    x_own = take(x_low).astype(F32)
-    dy_own = take(cotangent[0]).astype(F32) * scale
-    attn_own = scatter_sum(nn_dot(mixed, w_output))
-    hidden = x_own + attn_own
-    inv_two = lax.rsqrt(jnp.mean(hidden * hidden, axis=-1, keepdims=True) + EPSILON)
-    unit_two = hidden * inv_two
-    normed_two = gather_rows(unit_two * ffn_gain)
+    half_rows = jax.ShapeDtypeStruct((rows // 2, width), F32)
+    gain_row = jax.ShapeDtypeStruct((1, width), F32)
+    ffn_row, attn_row = ffn_gain[None, :], attn_gain[None, :]
+    attn_part = nn_dot(mixed, w_output).astype(BF16)
+    normed_two, hidden = line_sum(
+        [attn_part], [own_hidden], [x_low, ffn_row], [half_rows], 1
+    )
 
     dscaled = cotangent[0].astype(F32) * scale
     dffn = (keep * dscaled).astype(BF16)
@@ -435,16 +600,19 @@
     acted = (silu_gate * upward).astype(BF16)
     dgate = (dacted * upward * sigmoid_gate * (1.0 + gate * (1.0 - sigmoid_gate))).astype(BF16)
     dupward = (dacted * silu_gate).astype(BF16)
-    dnormed_own = scatter_sum(contract_cols(dgate, w_gate) + contract_cols(dupward, w_up))
-    ffn_own = scatter_sum(nn_dot(acted, w_down))
+    dnormed_part = (contract_cols(dgate, w_gate) + contract_cols(dupward, w_up)).astype(BF16)
+    ffn_part = nn_dot(acted, w_down).astype(BF16)
     total = lambda g: sum_plane(g, dp_size, ctx_size)
     grad_down = total(contract_rows(acted, dffn))
     grad_gate = total(contract_rows(normed_two, dgate))
     grad_up = total(contract_rows(normed_two, dupward))
-    grad_ffn_gain = jnp.sum(dnormed_own * unit_two, axis=0)
-    dhidden = norm_back(dnormed_own, unit_two, inv_two, ffn_gain)
-    dattn = gather_rows(keep * dy_own + dhidden)
-    output = gather_rows(x_own + keep * (attn_own + ffn_own))
+    dattn, dhidden, grad_ffn_gain = line_sum(
+        [dnormed_part],
+        [own_dhidden],
+        [hidden, cotangent[0], ffn_row, (keep * scale)[None]],
+        [half_rows, gain_row],
+        2,
+    )
     grad_output = total(contract_rows(mixed, dattn))
     dmixed = contract_cols(dattn, w_output).astype(BF16)
 
@@ -463,21 +631,24 @@
     dk_own = collect(dkeys).reshape(rows, kv_local, HEAD_DIM)
     dk_proj = rotate_back(dk_own, cosine, sine).reshape(rows, -1).astype(BF16)
     dv_proj = collect(dvalues).astype(BF16)
-    dnormed_one = scatter_sum(
+    dnormed_one = (
         contract_cols(dq_proj, w_query)
         + contract_cols(dk_proj, w_key)
         + contract_cols(dv_proj, w_value)
-    )
+    ).astype(BF16)
     grad_query = total(contract_rows(normed_one, dq_proj))
     grad_key = total(contract_rows(normed_one, dk_proj))
     grad_value = total(contract_rows(normed_one, dv_proj))
-    inv_own = take(inv_one)
-    unit_own = x_own * inv_own
-    grad_attn_gain = jnp.sum(dnormed_one * unit_own, axis=0)
+    through, output, grad_attn_gain = line_sum(
+        [dnormed_one, ffn_part],
+        [own_dinput, own_output],
+        [x_low, hidden, dhidden, attn_row, keep[None]],
+        [gain_row],
+        3,
+    )
     grad_attn_gain, grad_ffn_gain = lax.psum(
-        (grad_attn_gain, grad_ffn_gain), ("dp", "ctx", "tensor")
-    )
-    through = gather_rows(dhidden + norm_back(dnormed_one, unit_own, inv_own, attn_gain))
+        (grad_attn_gain[0], grad_ffn_gain[0]), ("dp", "ctx", "tensor")
+    )
     input_grad = dscaled + through.astype(F32)
     return (
         output.reshape(inputs.shape),

time: 933 us -> 2440 us (2.62)
  Pallas kernels: 50.7 us -> 1910 us
  waiting for transfers between devices: 448 us -> 134 us
  other arithmetic: 130 us -> 98.2 us
    pallas_call x0 -> x3, Pallas kernels: none -> 1870 us  [line_sum(): pl.pallas_call(functools.partial(line_kernel, size, chunk, streams, owner...]
    all_gather x4 -> x0, waiting for transfers between devices: 159 us -> none  [gather_rows(): return lax.all_gather(part.astype(BF16), 'tensor', axis=0, tiled=True)]
    reduce_scatter x4 -> x0, waiting for transfers between devices: 151 us -> none  [scatter_sum(): lax.psum_scatter(part.astype(BF16), 'tensor', scatter_dimension=0, tiled=...]
  transfers between devices with their start and end apart: 54 -> 46, of which waited for: 26 -> 16; matrix products, arithmetic and copies ran while one was open for 20% -> 7% of each run, Pallas kernels for 0% -> 38%
where the time goes in v2:
time: 2440 us; the launch traced here: 2430 us
  Pallas kernels  1910 us (78%)
  matrix products  151 us (6%)
  waiting for transfers between devices  134 us (5%)
  other arithmetic  98.2 us (4%)
  starting transfers between devices  51.5 us (2%)
  local copies, waits for them, and re-layouts  41.2 us (2%)
  blocking collectives  40.4 us (2%)
    pallas_call x3, Pallas kernels, line_sum(): pl.pallas_call(functools.partial(line_kernel, size, chunk, streams, owner...  1870 us
    ppermute x21, waiting for transfers between devices, sum_plane(): lax.ppermute(sent, ('dp', 'ctx'), perm).astype(F32)  75.1 us
    ppermute x21, waiting for transfers between devices, sum_plane(): other = lax.ppermute(pieces, ('dp', 'ctx'), perm)  59 us
    dot_general x7, matrix products, nn_dot(): return jnp.dot(left, right, preferred_element_type=F32)  58.4 us
    dot_general x7, matrix products, contract_cols(): return jnp.einsum('rc,dc->rd', left, right, preferred_element_type=F32)  52.1 us
  transfers between devices with their start and end apart: 46, of which 16 were waited for; matrix products, arithmetic and copies ran while one was open for 7% of the time, Pallas kernels for 38%

profile of v2, /device:TPU:0, one launch (start us, length us, event | category | flops | bytes accessed | tf_op | source)
XLA Modules:
  0.0 2428.6 jit_solution(2650445217171240728)
XLA Ops:
  35.1 11.8 fusion.14
  63.4 16.8 shard_map.230
  84.6 470.7 %shard_map.231 = (bf16[1024,2048]{1,0:T(8,128)(2,1)}, f32[512,2048]{1,0:T(8,128)}) custom-call(bf16[1024,2048]{1,0:T(8,128)(2,1)} %convolution_convert_fusion.1.refs_0_, bf16[1024,2048]{1,0:T(8,128)(2,1)} %bitcast.83, f32[1,2048]{1,0:T(1,128)} %bitcast.97), custom_call_target="tpu_custom_call" | custom-call | flops 2097152 | bytes 314572800 | tf_op jit(solution)/shard_map/pallas_call | solution.py:436
  555.4 12.0 fusion.36
  567.4 16.1 multiply_convert_fusion.2
  583.5 10.4 fusion.37
  594.0 10.5 add_convert_fusion.1.refs_0_
  604.4 472.5 %shard_map.232 = (bf16[1024,2048]{1,0:T(8,128)(2,1)}, f32[512,2048]{1,0:T(8,128)}, f32[1,2048]{1,0:T(1,128)}) custom-call(bf16[1024,2048]{1,0:T(8,128)(2,1)} %add_convert_fusion.1.refs_0_, f32[512,2048]{1,0:T(8,128)} %get-tuple-element.26.refs_1_.refs_3_, bf16[1024,2048]{1,0:T(8,128)(2,1)} %bitcast.85, f32[1,2048]{1,0:T(1,128)} %bitcast.98, f32[1]{0:T(128)} %bitcast.17.refs_4_), custom_call_target="tpu_custom_call" | custom-call | flops 2097152 | bytes 314572800 | tf_op jit(solution)/shard_map/pallas_call | solution.py:436
  1084.2 12.4 convolution_convert_fusion.refs_1_
  1096.5 9.1 fusion.13
  1114.5 9.5 fusion.41
  1124.0 22.8 shard_map.233
  1194.7 924.4 %shard_map.234 = (bf16[1024,2048]{1,0:T(8,128)(2,1)}, bf16[1024,2048]{1,0:T(8,128)(2,1)}, f32[1,2048]{1,0:T(1,128)}) custom-call(bf16[1024,2048]{1,0:T(8,128)(2,1)} %add_convert_fusion.refs_0_, bf16[1024,2048]{1,0:T(8,128)(2,1)} %convolution_convert_fusion.refs_1_, bf16[1024,2048]{1,0:T(8,128)(2,1)} %bitcast.84, ...), custom_call_target="tpu_custom_call" | custom-call | flops 4194304 | bytes 629145600 | tf_op jit(solution)/shard_map/pallas_call | solution.py:436
  2119.1 40.4 %all-reduce = (f32[2048]{0:T(1024)}, f32[2048]{0:T(1024)}) all-reduce(f32[2048]{0:T(1024)} %bitcast.101, f32[2048]{0:T(1024)S(1)} %bitcast.100), channel_id=1, replica_groups=mesh['dp'=4,'ctx'=2,'tensor'=4] {'dp','ctx','tensor'}, use_global_device_ids=true, to_apply=%region_2.3 | all-reduce | flops 4096 | bytes 32768 | tf_op jit(solution)/shard_map/psum | solution.py:649
  2224.1 11.2 collective-permute-done.41
  2236.0 14.8 collective-permute-done.29
  2252.9 21.1 collective-permute-done.35
  2301.1 15.3 collective-permute-done.31
  2325.1 10.8 collective-permute-done.37
  2340.5 12.2 collective-permute-done.20
  2362.4 11.4 collective-permute-done.26
  2395.8 9.6 fusion.5
  2405.3 10.1 fusion.3
  2415.4 9.8 fusion.4
  (293 shorter events, 258.4 us)
Async XLA Ops:
  7.7 47.1 %collective-permute-start.1 = (bf16[1024,256]{1,0:T(8,128)(2,1)}, bf16[1024,256]{1,0:T(8,128)(2,1)}, u32[]{:S(2)}, u32[]{:S(2)}) collective-permute-start(bf16[1024,256]{1,0:T(8,128)(2,1)} %convolution_convert_fusion.3), channel_id=1, source_target_pairs={{0,4},{4,0},{1,5},{5,1},{2,6},{6,2},{3,7},{7,3},{8,12},{12,8},{9,1... | collective-permute-start | bytes 1572872 | tf_op jit(solution)/shard_map/ppermute | solution.py:530
  21.3 28.9 %collective-permute-start = (bf16[1024,256]{0,1:T(8,128)(2,1)}, bf16[1024,256]{0,1:T(8,128)(2,1)}, u32[]{:S(2)}, u32[]{:S(2)}) collective-permute-start(bf16[1024,256]{0,1:T(8,128)(2,1)} %bitcast.14), channel_id=1, source_target_pairs={{0,4},{4,0},{1,5},{5,1},{2,6},{6,2},{3,7},{7,3},{8,12},{12,8},{9,1... | collective-permute-start | bytes 1572872 | tf_op jit(solution)/shard_map/ppermute | solution.py:530
  1147.7 34.5 %collective-permute-start.3 = (bf16[1024,256]{1,0:T(8,128)(2,1)}, bf16[1024,256]{1,0:T(8,128)(2,1)}, u32[]{:S(2)}, u32[]{:S(2)}) collective-permute-start(bf16[1024,256]{1,0:T(8,128)(2,1)} %slice.80), channel_id=1, source_target_pairs={{0,4},{4,0},{1,5},{5,1},{2,6},{6,2},{3,7},{7,3},{8,12},{12,8},{9,1... | collective-permute-start | bytes 1572872 | tf_op jit(solution)/shard_map/ppermute | solution.py:628
  1149.2 23.7 collective-permute-start.2
  1150.9 1018.9 %collective-permute-start.22 = (bf16[256,2048]{1,0:T(8,128)(2,1)}, bf16[256,2048]{1,0:T(8,128)(2,1)}, u32[]{:S(2)}, u32[]{:S(2)}) collective-permute-start(bf16[256,2048]{1,0:T(8,128)(2,1)} %dynamic-slice_convert_fusion.3), channel_id=1, source_target_pairs={{0,8},{4,12},{8,0},{12,4},{16,24},{20,28},{24,16},{28,20},{1,9},{5... | collective-permute-start | bytes 3145736 | tf_op jit(solution)/shard_map/ppermute | solution.py:295
  1154.9 1019.8 %collective-permute-start.4 = (bf16[1024,512]{1,0:T(8,128)(2,1)}, bf16[1024,512]{1,0:T(8,128)(2,1)}, u32[]{:S(2)}, u32[]{:S(2)}) collective-permute-start(bf16[1024,512]{1,0:T(8,128)(2,1)} %dynamic-slice_convert_fusion.4), channel_id=1, source_target_pairs={{0,8},{4,12},{8,0},{12,4},{16,24},{20,28},{24,16},{28,20},{1,9},{5... | collective-permute-start | bytes 3145736 | tf_op jit(solution)/shard_map/ppermute | solution.py:295
  1160.0 1049.5 %collective-permute-start.40 = (bf16[704,2048]{1,0:T(8,128)(2,1)}, bf16[704,2048]{1,0:T(8,128)(2,1)}, u32[]{:S(2)}, u32[]{:S(2)}) collective-permute-start(bf16[704,2048]{1,0:T(8,128)(2,1)} %dynamic-slice_convert_fusion), channel_id=1, source_target_pairs={{0,8},{4,12},{8,0},{12,4},{16,24},{20,28},{24,16},{28,20},{1,9},{5... | collective-permute-start | bytes 8650760 | tf_op jit(solution)/shard_map/ppermute | solution.py:295
  1172.9 1043.2 %collective-permute-start.28 = (bf16[1024,1408]{1,0:T(8,128)(2,1)}, bf16[1024,1408]{1,0:T(8,128)(2,1)}, u32[]{:S(2)}, u32[]{:S(2)}) collective-permute-start(bf16[1024,1408]{1,0:T(8,128)(2,1)} %dynamic-slice_convert_fusion.2), channel_id=1, source_target_pairs={{0,8},{4,12},{8,0},{12,4},{16,24},{20,28},{24,16},{28,20},{1,9},{5... | collective-permute-start | bytes 8650760 | tf_op jit(solution)/shard_map/ppermute | solution.py:295
  1182.2 989.5 %collective-permute-start.10 = (bf16[1024,256]{1,0:T(8,128)(2,1)S(1)}, bf16[1024,256]{1,0:T(8,128)(2,1)S(1)}, u32[]{:S(2)}, u32[]{:S(2)}) collective-permute-start(bf16[1024,256]{1,0:T(8,128)(2,1)S(1)} %dynamic-slice_convert_fusion.6), channel_id=1, source_target_pairs={{0,8},{4,12},{8,0},{12,4},{16,24},{20,28},{24,16},{28,20},{1,9},{5... | collective-permute-start | bytes 1572872 | tf_op jit(solution)/shard_map/ppermute | solution.py:295
  2171.7 29.4 %collective-permute-start.23 = (bf16[128,2048]{1,0:T(8,128)(2,1)S(1)}, bf16[128,2048]{1,0:T(8,128)(2,1)S(1)}, u32[]{:S(2)}, u32[]{:S(2)}) collective-permute-start(bf16[128,2048]{1,0:T(8,128)(2,1)S(1)} %constant_dynamic-slice_fusion.7), channel_id=1, source_target_pairs={{0,4},{4,0},{8,24},{12,28},{16,20},{20,16},{24,8},{28,12},{1,5},{5... | collective-permute-start | bytes 1572872 | tf_op jit(solution)/shard_map/ppermute | solution.py:295
  2203.9 115.5 %collective-permute-start.24 = (bf16[64,2048]{1,0:T(8,128)(2,1)}, bf16[64,2048]{1,0:T(8,128)(2,1)}, u32[]{:S(2)}, u32[]{:S(2)}) collective-permute-start(bf16[64,2048]{1,0:T(8,128)(2,1)} %constant_dynamic-slice_fusion.6), channel_id=1, source_target_pairs={{0,16},{4,20},{8,12},{12,8},{16,0},{20,4},{24,28},{28,24},{1,17},{... | collective-permute-start | bytes 786440 | tf_op jit(solution)/shard_map/ppermute | solution.py:295
  2206.7 113.8 %collective-permute-start.14 = (bf16[512,256]{1,0:T(8,128)(2,1)}, bf16[512,256]{1,0:T(8,128)(2,1)}, u32[]{:S(2)}, u32[]{:S(2)}) collective-permute-start(bf16[512,256]{1,0:T(8,128)(2,1)} %maximum_select_fusion.19), channel_id=1, source_target_pairs={{0,4},{4,0},{8,24},{12,28},{16,20},{20,16},{24,8},{28,12},{1,5},{5... | collective-permute-start | bytes 786440 | tf_op jit(solution)/shard_map/ppermute | solution.py:300
  2209.5 114.5 %collective-permute-start.6 = (bf16[256,512]{1,0:T(8,128)(2,1)}, bf16[256,512]{1,0:T(8,128)(2,1)}, u32[]{:S(2)}, u32[]{:S(2)}) collective-permute-start(bf16[256,512]{1,0:T(8,128)(2,1)} %constant_dynamic-slice_fusion.12), channel_id=1, source_target_pairs={{0,16},{4,20},{8,12},{12,8},{16,0},{20,4},{24,28},{28,24},{1,17},{... | collective-permute-start | bytes 786440 | tf_op jit(solution)/shard_map/ppermute | solution.py:295
  2221.6 29.2 %collective-permute-start.29 = (bf16[512,1408]{1,0:T(8,128)(2,1)}, bf16[512,1408]{1,0:T(8,128)(2,1)S(1)}, u32[]{:S(2)}, u32[]{:S(2)}) collective-permute-start(bf16[512,1408]{1,0:T(8,128)(2,1)} %constant_dynamic-slice_fusion.5), channel_id=1, source_target_pairs={{0,4},{4,0},{8,24},{12,28},{16,20},{20,16},{24,8},{28,12},{1,5},{5... | collective-permute-start | bytes 4325384 | tf_op jit(solution)/shard_map/ppermute | solution.py:295
  2235.3 38.6 %collective-permute-start.35 = (bf16[512,1408]{1,0:T(8,128)(2,1)S(1)}, bf16[512,1408]{1,0:T(8,128)(2,1)S(1)}, u32[]{:S(2)}, u32[]{:S(2)}) collective-permute-start(bf16[512,1408]{1,0:T(8,128)(2,1)S(1)} %constant_dynamic-slice_fusion.3), channel_id=1, source_target_pairs={{0,4},{4,0},{8,24},{12,28},{16,20},{20,16},{24,8},{28,12},{1,5},{5... | collective-permute-start | bytes 4325384 | tf_op jit(solution)/shard_map/ppermute | solution.py:295
  2250.8 25.2 %collective-permute-start.42 = (bf16[176,2048]{1,0:T(8,128)(2,1)S(1)}, bf16[176,2048]{1,0:T(8,128)(2,1)S(1)}, u32[]{:S(2)}, u32[]{:S(2)}) collective-permute-start(bf16[176,2048]{1,0:T(8,128)(2,1)S(1)} %constant_dynamic-slice_fusion), channel_id=1, source_target_pairs={{0,16},{4,20},{8,12},{12,8},{16,0},{20,4},{24,28},{28,24},{1,17},{... | collective-permute-start | bytes 2162696 | tf_op jit(solution)/shard_map/ppermute | solution.py:295
  2300.9 37.8 %collective-permute-start.44 = (bf16[352,2048]{1,0:T(8,128)(2,1)S(1)}, bf16[352,2048]{1,0:T(8,128)(2,1)S(1)}, u32[]{:S(2)}, u32[]{:S(2)}) collective-permute-start(bf16[352,2048]{1,0:T(8,128)(2,1)S(1)} %maximum_select_fusion.10), channel_id=1, source_target_pairs={{0,4},{4,0},{8,24},{12,28},{16,20},{20,16},{24,8},{28,12},{1,5},{5... | collective-permute-start | bytes 4325384 | tf_op jit(solution)/shard_map/ppermute | solution.py:300
  2319.4 36.9 %collective-permute-start.32 = (bf16[512,1408]{1,0:T(8,128)(2,1)S(1)}, bf16[512,1408]{1,0:T(8,128)(2,1)S(1)}, u32[]{:S(2)}, u32[]{:S(2)}) collective-permute-start(bf16[512,1408]{1,0:T(8,128)(2,1)S(1)} %maximum_select_fusion.8), channel_id=1, source_target_pairs={{0,4},{4,0},{8,24},{12,28},{16,20},{20,16},{24,8},{28,12},{1,5},{5... | collective-permute-start | bytes 4325384 | tf_op jit(solution)/shard_map/ppermute | solution.py:300
  2320.5 32.2 %collective-permute-start.20 = (bf16[512,256]{1,0:T(8,128)(2,1)S(1)}, bf16[512,256]{1,0:T(8,128)(2,1)S(1)}, u32[]{:S(2)}, u32[]{:S(2)}) collective-permute-start(bf16[512,256]{1,0:T(8,128)(2,1)S(1)} %copy-done.32), channel_id=1, source_target_pairs={{0,4},{4,0},{8,24},{12,28},{16,20},{20,16},{24,8},{28,12},{1,5},{5... | collective-permute-start | bytes 786440 | tf_op jit(solution)/shard_map/ppermute | solution.py:300
  2324.0 31.8 %collective-permute-start.25 = (bf16[64,2048]{1,0:T(8,128)(2,1)S(1)}, bf16[64,2048]{1,0:T(8,128)(2,1)S(1)}, u32[]{:S(2)}, u32[]{:S(2)}) collective-permute-start(bf16[64,2048]{1,0:T(8,128)(2,1)S(1)} %add_convert_fusion.19), channel_id=1, source_target_pairs={{0,16},{4,20},{8,12},{12,8},{16,0},{20,4},{24,28},{28,24},{1,17},{... | collective-permute-start | bytes 786440 | tf_op jit(solution)/shard_map/ppermute | solution.py:300
  2338.7 43.8 %collective-permute-start.38 = (bf16[512,1408]{1,0:T(8,128)(2,1)S(1)}, bf16[512,1408]{1,0:T(8,128)(2,1)S(1)}, u32[]{:S(2)}, u32[]{:S(2)}) collective-permute-start(bf16[512,1408]{1,0:T(8,128)(2,1)S(1)} %maximum_select_fusion.9), channel_id=1, source_target_pairs={{0,4},{4,0},{8,24},{12,28},{16,20},{20,16},{24,8},{28,12},{1,5},{5... | collective-permute-start | bytes 4325384 | tf_op jit(solution)/shard_map/ppermute | solution.py:300
  2352.7 43.0 %collective-permute-start.45 = (bf16[704,2048]{1,0:T(8,128)(2,1)S(1)}, bf16[704,2048]{1,0:T(8,128)(2,1)S(1)}, u32[]{:S(2)}, u32[]{:S(2)}) collective-permute-start(bf16[704,2048]{1,0:T(8,128)(2,1)S(1)} %maximum_select_fusion.5), channel_id=1, source_target_pairs={{0,8},{4,12},{8,0},{12,4},{16,24},{20,28},{24,16},{28,20},{1,9},{5... | collective-permute-start | bytes 8650760 | tf_op jit(solution)/shard_map/ppermute | solution.py:300
  2373.8 31.5 %collective-permute-start.33 = (bf16[1024,1408]{1,0:T(8,128)(2,1)S(1)}, bf16[1024,1408]{1,0:T(8,128)(2,1)S(1)}, u32[]{:S(2)}, u32[]{:S(2)}) collective-permute-start(bf16[1024,1408]{1,0:T(8,128)(2,1)S(1)} %maximum_select_fusion.3), channel_id=1, source_target_pairs={{0,8},{4,12},{8,0},{12,4},{16,24},{20,28},{24,16},{28,20},{1,9},{5... | collective-permute-start | bytes 8650760 | tf_op jit(solution)/shard_map/ppermute | solution.py:300
  2386.6 28.8 %collective-permute-start.39 = (bf16[1024,1408]{1,0:T(8,128)(2,1)S(1)}, bf16[1024,1408]{1,0:T(8,128)(2,1)S(1)}, u32[]{:S(2)}, u32[]{:S(2)}) collective-permute-start(bf16[1024,1408]{1,0:T(8,128)(2,1)S(1)} %maximum_select_fusion.4), channel_id=1, source_target_pairs={{0,8},{4,12},{8,0},{12,4},{16,24},{20,28},{24,16},{28,20},{1,9},{5... | collective-permute-start | bytes 8650760 | tf_op jit(solution)/shard_map/ppermute | solution.py:300
  (72 other events, 1901.5 us)

commit v3 on v2

--- a/solution.py
+++ b/solution.py
@@ -248,73 +248,33 @@
     )
 
 
-def fold_steps(dp_size, ctx_size):
+LINE_CHUNK = 32
+LINE_WINDOW = 2
+LINE_SKEW = 2
+MESH_AXES = ("dp", "ctx", "tensor")
+
+
+def pair_steps(sizes):
     steps = []
-    bit = 1
-    while bit < ctx_size:
-        steps.append(("ctx", bit))
-        bit *= 2
-    along = []
-    bit = 2
-    while bit < dp_size:
-        along.append(("dp", bit))
-        bit *= 2
-    even, odd = steps + along, along + steps
-    plan = [((("dp", 1)), (("dp", 1)))] if dp_size > 1 else []
-    return plan + list(zip(even, odd))
-
-
-def step_perm(step, dp_size, ctx_size):
-    pairs = []
-    for d in range(dp_size):
-        for c in range(ctx_size):
-            axis, bit = step[d % 2]
-            other = (d ^ bit, c) if axis == "dp" else (d, c ^ bit)
-            pairs.append((d * ctx_size + c, other[0] * ctx_size + other[1]))
-    return pairs
-
-
-def step_bit(step):
-    d, c = lax.axis_index("dp"), lax.axis_index("ctx")
-
-    def of(axis, bit):
-        return jnp.where(((d if axis == "dp" else c) & bit) != 0, 1, 0)
-
-    return jnp.where(d % 2 == 0, of(*step[0]), of(*step[1]))
-
-
-def sum_plane(grad, dp_size, ctx_size):
-    plan = fold_steps(dp_size, ctx_size)
-    pieces = grad
-    perms = [step_perm(s, dp_size, ctx_size) for s in plan]
-    bits = [step_bit(s) for s in plan]
-    for perm, bit in zip(perms, bits):
-        half = pieces.shape[0] // 2
-        kept = lax.dynamic_slice_in_dim(pieces, bit * half, half, 0)
-        sent = lax.dynamic_slice_in_dim(pieces, (1 - bit) * half, half, 0).astype(BF16)
-        pieces = kept.astype(F32) + lax.ppermute(sent, ("dp", "ctx"), perm).astype(F32)
-        if perm is not perms[-1]:
-            pieces = pieces.astype(BF16)
-    pieces = pieces.astype(BF16)
-    for perm, bit in zip(perms[::-1], bits[::-1]):
-        other = lax.ppermute(pieces, ("dp", "ctx"), perm)
-        pieces = jnp.where(
-            bit == 0,
-            jnp.concatenate([pieces, other], 0),
-            jnp.concatenate([other, pieces], 0),
-        )
-    return pieces.astype(F32)
-
-
-LINE_CHUNK = 32
-
-
-def line_kernel(size, chunk, streams, owners, side_count, out_count, *refs):
+    for axis, size in zip(MESH_AXES, sizes):
+        bit = 1
+        while bit < size:
+            steps.append((axis, bit))
+            bit *= 2
+    return steps
+
+
+def partner(axis, bit):
+    index = lax.axis_index(axis)
+    return jnp.where((index // bit) % 2 == 0, index + bit, index - bit)
+
+
+def line_kernel(size, chunk, streams, owners, pairs, side_count, out_count, *refs):
     parts, refs = refs[:streams], refs[streams:]
     sides, refs = refs[:side_count], refs[side_count:]
     shared, refs = refs[:streams], refs[streams:]
     kept, refs = refs[:out_count], refs[out_count:]
-    inbox, send_up, recv_up, send_back, recv_back = refs
+    inbox, send_up, recv_up, send_back, recv_back = refs[:5]
     half = parts[0].shape[0] // 2
     count = half // chunk
     last = size - 1
@@ -324,14 +284,23 @@
 
     barrier = pltpu.get_barrier_semaphore()
 
-    def greet(other):
+    def greet(axis, other):
         pl.semaphore_signal(
-            barrier, inc=1, device_id={"tensor": other}, device_id_type=pl.DeviceIdType.MESH
+            barrier, inc=1, device_id={axis: other}, device_id_type=pl.DeviceIdType.MESH
         )
 
-    pl.when(me < last)(lambda: greet(above))
-    pl.when(me > 0)(lambda: greet(below))
-    pl.semaphore_wait(barrier, jnp.where((me > 0) & (me < last), 2, 1))
+    if pairs:
+        for axis, bit in pairs:
+            greet(axis, partner(axis, bit))
+        far_above = jnp.where(me % 2 == 0, 0, 1) * jnp.where(me < last, 1, 0)
+        far_below = jnp.where(me % 2 == 0, 1, 0) * jnp.where(me > 0, 1, 0)
+        pl.when(far_above == 1)(lambda: greet("tensor", above))
+        pl.when(far_below == 1)(lambda: greet("tensor", below))
+        pl.semaphore_wait(barrier, len(pairs) + far_above + far_below)
+    else:
+        pl.when(me < last)(lambda: greet("tensor", above))
+        pl.when(me > 0)(lambda: greet("tensor", below))
+        pl.semaphore_wait(barrier, jnp.where((me > 0) & (me < last), 2, 1))
 
     def place(f, i):
         return pl.ds(pl.multiple_of(f * half + i * chunk, chunk), chunk)
@@ -367,6 +336,7 @@
 
         @pl.when(position == 0)
         def _():
+            pl.when(i >= LINE_WINDOW)(lambda: onward(k, f, i - LINE_WINDOW, mine).wait_send())
             onward(k, f, i, mine).start()
 
         @pl.when(position > 0)
@@ -394,27 +364,30 @@
             pl.when(position > 0)(lambda: backward(k, f, i).start())
 
     def step(s, carry):
-        @pl.when(s < count)
-        def _():
-            for k in range(streams):
-                for f in range(2):
-                    reduce_chunk(k, f, s)
-
         for k in range(streams):
             for f in range(2):
-                pass_back(k, f, s - 2 * (last - flows[f][0]))
+                i = s - LINE_SKEW * flows[f][0]
+                pl.when((i >= 0) & (i < count))(lambda: reduce_chunk(k, f, i))
+        for k in range(streams):
+            for f in range(2):
+                pass_back(k, f, s - LINE_SKEW * (2 * last - flows[f][0]))
         return carry
 
-    for ref in kept:
-        if ref.shape[0] == 1:
+    if not pairs:
+        for ref in kept[1:]:
             ref[...] = jnp.zeros_like(ref)
-    lax.fori_loop(0, count + 2 * last, step, 0)
+    else:
+        gains = kept[0]
+        gains[...] = jnp.zeros_like(gains)
+        gains[1:2, :] = sides[-1][...]
+    lax.fori_loop(0, count + 2 * LINE_SKEW * last, step, 0)
 
     def drain(i, carry):
         for k in range(streams):
             for f in range(2):
                 position = flows[f][0]
-                pl.when(position < last)(
+                waited = (position == 0) & (i < count - LINE_WINDOW)
+                pl.when((position < last) & ~waited)(
                     lambda: onward(k, f, i, inbox.at[k, f, local(i)]).wait_send()
                 )
                 pl.when(position > 0)(lambda: backward(k, f, i).wait_send())
@@ -422,8 +395,25 @@
 
     lax.fori_loop(0, count, drain, 0)
 
-
-def line_sum(parts, owners, sides, kept, collective_id):
+    if pairs:
+        slots, sums, send_pair, recv_pair = refs[5:]
+        sums[0] = gains[...]
+        for n, (axis, bit) in enumerate(pairs):
+            copy = pltpu.make_async_remote_copy(
+                src_ref=sums.at[n],
+                dst_ref=slots.at[n],
+                send_sem=send_pair.at[n],
+                recv_sem=recv_pair.at[n],
+                device_id={axis: partner(axis, bit)},
+                device_id_type=pl.DeviceIdType.MESH,
+            )
+            copy.start()
+            copy.wait()
+            sums[n + 1] = sums[n] + slots[n]
+        gains[...] = sums[len(pairs)]
+
+
+def line_sum(parts, owners, sides, kept, collective_id, pairs=()):
     rows, width = parts[0].shape
     size = lax.axis_size("tensor")
     streams = len(parts)
@@ -433,12 +423,23 @@
     scalar = pl.BlockSpec(memory_space=pltpu.SMEM)
     sems = pltpu.SemaphoreType.DMA((streams, 2, count))
     outs = [jax.ShapeDtypeStruct((rows, width), BF16)] * streams + list(kept)
+    extra = []
+    if pairs:
+        pair_sems = pltpu.SemaphoreType.DMA((len(pairs),))
+        extra = [
+            pltpu.VMEM((len(pairs), 8, width), F32),
+            pltpu.VMEM((len(pairs) + 1, 8, width), F32),
+            pair_sems,
+            pair_sems,
+        ]
     return pl.pallas_call(
-        functools.partial(line_kernel, size, chunk, streams, owners, len(sides), len(kept)),
+        functools.partial(
+            line_kernel, size, chunk, streams, owners, pairs, len(sides), len(kept)
+        ),
         out_shape=outs,
         in_specs=[whole] * streams + [scalar if s.ndim == 1 else whole for s in sides],
         out_specs=[whole] * len(outs),
-        scratch_shapes=[pltpu.VMEM((streams, 2, rows // 2, width), BF16)] + [sems] * 4,
+        scratch_shapes=[pltpu.VMEM((streams, 2, rows // 2, width), BF16)] + [sems] * 4 + extra,
         compiler_params=pltpu.CompilerParams(
             collective_id=collective_id, has_side_effects=True, vmem_limit_bytes=56 * 2**20
         ),
@@ -463,7 +464,7 @@
 
 
 def own_dhidden(total, where, here, sides, kept):
-    hidden_ref, cot_ref, gain_ref, factor = sides
+    x_ref, hidden_ref, cot_ref, gain_ref, factor = sides
     unit, inverse = unit_of(hidden_ref[here, :])
     kept[1][...] += jnp.sum(total * unit, axis=0, keepdims=True)
     dhidden = norm_back(total, unit, inverse, gain_ref[...])
@@ -471,17 +472,17 @@
     return cot_ref[where, :].astype(F32) * factor[0] + dhidden
 
 
+def own_output(total, where, here, sides, kept):
+    x_ref, hidden_ref, cot_ref, gain_ref, factor = sides
+    x = x_ref[where, :].astype(F32)
+    return x + factor[1] * ((hidden_ref[here, :] - x) + total)
+
+
 def own_dinput(total, where, here, sides, kept):
-    x_ref, hidden_ref, dhidden_ref, gain_ref, factor = sides
+    x_ref, dhidden_ref, gain_ref, _ = sides
     unit, inverse = unit_of(x_ref[where, :].astype(F32))
-    kept[0][...] += jnp.sum(total * unit, axis=0, keepdims=True)
+    kept[0][0:1, :] += jnp.sum(total * unit, axis=0, keepdims=True)
     return dhidden_ref[here, :] + norm_back(total, unit, inverse, gain_ref[...])
-
-
-def own_output(total, where, here, sides, kept):
-    x_ref, hidden_ref, dhidden_ref, gain_ref, factor = sides
-    x = x_ref[where, :].astype(F32)
-    return x + factor[0] * ((hidden_ref[here, :] - x) + total)
 
 
 def sequence_positions(order_row, length):
@@ -602,18 +603,24 @@
     dupward = (dacted * silu_gate).astype(BF16)
     dnormed_part = (contract_cols(dgate, w_gate) + contract_cols(dupward, w_up)).astype(BF16)
     ffn_part = nn_dot(acted, w_down).astype(BF16)
-    total = lambda g: sum_plane(g, dp_size, ctx_size)
-    grad_down = total(contract_rows(acted, dffn))
-    grad_gate = total(contract_rows(normed_two, dgate))
-    grad_up = total(contract_rows(normed_two, dupward))
-    dattn, dhidden, grad_ffn_gain = line_sum(
-        [dnormed_part],
-        [own_dhidden],
-        [hidden, cotangent[0], ffn_row, (keep * scale)[None]],
+    total = lambda g, *axes: lax.psum(g, axes)
+    ffn_grads = (
+        contract_rows(acted, dffn).astype(BF16),
+        contract_rows(normed_two, dgate).astype(BF16),
+        contract_rows(normed_two, dupward).astype(BF16),
+    )
+    dnormed_part, ffn_part, ffn_grads = lax.optimization_barrier(
+        (dnormed_part, ffn_part, ffn_grads)
+    )
+    ffn_grads = total(ffn_grads, "dp", "ctx")
+    dattn, output, dhidden, ffn_gain_part = line_sum(
+        [dnormed_part, ffn_part],
+        [own_dhidden, own_output],
+        [x_low, hidden, cotangent[0], ffn_row, jnp.stack([keep * scale, keep])],
         [half_rows, gain_row],
         2,
     )
-    grad_output = total(contract_rows(mixed, dattn))
+    grad_output = contract_rows(mixed, dattn)
     dmixed = contract_cols(dattn, w_output).astype(BF16)
 
     dq_proj, dkeys, dvalues = attend_back(
@@ -636,19 +643,27 @@
         + contract_cols(dk_proj, w_key)
         + contract_cols(dv_proj, w_value)
     ).astype(BF16)
-    grad_query = total(contract_rows(normed_one, dq_proj))
-    grad_key = total(contract_rows(normed_one, dk_proj))
-    grad_value = total(contract_rows(normed_one, dv_proj))
-    through, output, grad_attn_gain = line_sum(
-        [dnormed_one, ffn_part],
-        [own_dinput, own_output],
-        [x_low, hidden, dhidden, attn_row, keep[None]],
-        [gain_row],
+    attn_grads = (
+        contract_rows(normed_one, dq_proj).astype(BF16),
+        contract_rows(normed_one, dk_proj).astype(BF16),
+        contract_rows(normed_one, dv_proj).astype(BF16),
+        grad_output.astype(BF16),
+    )
+    dnormed_one, attn_grads = lax.optimization_barrier((dnormed_one, attn_grads))
+    attn_grads, ffn_grads = lax.optimization_barrier((attn_grads, ffn_grads))
+    attn_grads = total(attn_grads, "ctx", "dp")
+    pairs = pair_steps((dp_size, ctx_size, lax.axis_size("tensor")))
+    through, gains = line_sum(
+        [dnormed_one],
+        [own_dinput],
+        [x_low, dhidden, attn_row, ffn_gain_part],
+        [jax.ShapeDtypeStruct((8, width), F32)],
         3,
-    )
-    grad_attn_gain, grad_ffn_gain = lax.psum(
-        (grad_attn_gain[0], grad_ffn_gain[0]), ("dp", "ctx", "tensor")
-    )
+        tuple(pairs),
+    )
+    grad_attn_gain, grad_ffn_gain = gains[0], gains[1]
+    grad_down, grad_gate, grad_up = (g.astype(F32) for g in ffn_grads)
+    grad_query, grad_key, grad_value, grad_output = (g.astype(F32) for g in attn_grads)
     input_grad = dscaled + through.astype(F32)
     return (
         output.reshape(inputs.shape),

time: 2440 us -> 775 us (0.32)
  Pallas kernels: 1910 us -> 510 us
  waiting for transfers between devices: 134 us -> 9.6 us
  other arithmetic: 98.2 us -> 52.4 us
  starting transfers between devices: 51.5 us -> 6.46 us
  blocking collectives: 40.4 us -> 0 us
    pallas_call x3, Pallas kernels: 1870 us -> 476 us  [line_sum(): pl.pallas_call(functools.partial(line_kernel, size, chunk, streams, owner...]
    ppermute x42 -> x0, waiting for transfers between devices: 134 us -> none  [the longest x21 75.1 us: sum_plane(): lax.ppermute(sent, ('dp', 'ctx'), perm).astype(F32)]
    ppermute x42 -> x0, starting transfers between devices: 46.5 us -> none  [the longest x21 24.2 us: sum_plane(): other = lax.ppermute(pieces, ('dp', 'ctx'), perm)]
    psum x1 -> x0, blocking collectives: 40.4 us -> none  [per_device(): lax.psum((grad_attn_gain[0], grad_ffn_gain[0]), ('dp', 'ctx', 'tensor'))]
    convert_element_type x28 -> x7, other arithmetic: 55.6 us -> 29 us  [the longest x3 19.1 us: per_device(): grad_down, grad_gate, grad_up = (g.astype(F32) for g in ffn_grads)]
  transfers between devices with their start and end apart: 46 -> 6, of which waited for: 16 -> 1; matrix products, arithmetic and copies ran while one was open for 7% -> 14% of each run, Pallas kernels for 38% -> 49%
where the time goes in v3:
time: 775 us; the launch traced here: 769 us
  Pallas kernels  510 us (66%)
  matrix products  149 us (19%)
  other arithmetic  52.4 us (7%)
  local copies, waits for them, and re-layouts  23.6 us (3%)
  between operations  17.4 us (2%)
  waiting for transfers between devices  9.6 us (1%)
    pallas_call x3, Pallas kernels, line_sum(): pl.pallas_call(functools.partial(line_kernel, size, chunk, streams, owner...  476 us
    dot_general x7, matrix products, contract_cols(): return jnp.einsum('rc,dc->rd', left, right, preferred_element_type=F32)  56.3 us
    dot_general x7, matrix products, nn_dot(): return jnp.dot(left, right, preferred_element_type=F32)  50.4 us
    dot_general x7, matrix products, contract_rows(): return jnp.einsum('rd,rf->df', left, right, preferred_element_type=F32)  42.5 us
    pallas_call x1, Pallas kernels, attend_back(): pl.pallas_call(functools.partial(attend_back_kernel, group, span), grid_s...  19.6 us
    convert_element_type x3, other arithmetic, per_device(): grad_down, grad_gate, grad_up = (g.astype(F32) for g in ffn_grads)  19.1 us
  transfers between devices with their start and end apart: 6, of which 1 were waited for; matrix products, arithmetic and copies ran while one was open for 14% of the time, Pallas kernels for 49%

profile of v3, /device:TPU:0, one launch (start us, length us, event | category | flops | bytes accessed | tf_op | source)
XLA Modules:
  0.0 768.9 jit_solution(14957229062068724027)
XLA Ops:
  28.0 5.4 fusion.6
  36.6 10.3 %fusion.10 = f32[1024,1408]{1,0:T(8,128)} fusion(bf16[1408,2048]{1,0:T(8,128)(2,1)} %param.29, f32[]{:T(128)} %bitcast.2, f32[]{:T(128)} %bitcast, bf16[1,1024,2048]{2,1,0:T(8,128)(2,1)S(1)} %copy-done.14), kind=kOutput, calls=%fused_computation.27 | convolution fusion | flops 5913968640 | bytes 15728648 | tf_op jit(solution)/shard_map/rc,dc->rd/dot_general | solution.py:521
  62.1 14.2 %shard_map.230 = (bf16[1024,512]{1,0:T(8,128)(2,1)S(1)}, f32[2,2,1024]{2,1,0:T(2,128)S(1)}) custom-call(s32[2]{0:T(128)S(1)} %get-tuple-element.101.query_order, s32[4]{0:T(128)S(1)} %pad_add_fusion.key_order, bf16[1024,512]{1,0:T(8,128)(2,1)S(1)} %copy-done.4, bf16[2048,256]{1,0:T(8,128)(2,1)S(1)} %copy-done.6, bf16[256,2048]{1,0:T(8,128)(2,1)S(1)} %copy-done.8), custom_call_target="tpu_custom_call" | custom-call | flops 4294967296 | bytes 4194304 | tf_op jit(solution)/shard_map/pallas_call | solution.py:91
  80.7 116.6 %shard_map.231 = (bf16[1024,2048]{1,0:T(8,128)(2,1)}, f32[512,2048]{1,0:T(8,128)}) custom-call(bf16[1024,2048]{1,0:T(8,128)(2,1)} %convolution_convert_fusion.4.refs_0_, bf16[1024,2048]{1,0:T(8,128)(2,1)} %bitcast.85, f32[1,2048]{1,0:T(1,128)} %bitcast.102), custom_call_target="tpu_custom_call" | custom-call | flops 2097152 | bytes 314572800 | tf_op jit(solution)/shard_map/pallas_call | solution.py:435
  197.3 11.8 %fusion.28 = f32[1024,1408]{1,0:T(8,128)} fusion(bf16[1024,2048]{1,0:T(8,128)(2,1)} %get-tuple-element.42, bf16[2048,1408]{1,0:T(8,128)(2,1)} %param.27), kind=kOutput, calls=%fused_computation.80 | convolution fusion | flops 5905580032 | bytes 15728640 | tf_op jit(solution)/shard_map/dot_general | solution.py:27
  209.1 14.5 %multiply_convert_fusion.2 = (bf16[1024,1408]{1,0:T(8,128)(2,1)S(1)}, bf16[1024,1408]{1,0:T(8,128)(2,1)}, bf16[1024,1408]{1,0:T(8,128)(2,1)}) fusion(f32[1024,1408]{1,0:T(8,128)} %fusion.28, f32[1024,1408]{1,0:T(8,128)} %fusion.10, bf16[1024,2048]{1,0:T(8,128)(2,1)} %get-tuple-element.42, bf16[2048,1408]{1,0:T(8,128)(2,1)S(1)} %bitcast.113), kind=kOutput, calls=%fused_computation.14 | convolution fusion | flops 5927206912 | bytes 30146560 | tf_op jit(solution)/shard_map/dot_general | solution.py:27
  223.6 11.1 %convolution_convert_fusion.1 = bf16[2048,1408]{1,0:T(8,128)(2,1)} fusion(bf16[1024,2048]{1,0:T(8,128)(2,1)} %get-tuple-element.42, bf16[1024,1408]{1,0:T(8,128)(2,1)} %get-tuple-element.79), kind=kOutput, calls=%fused_computation.12 | convolution fusion | flops 5908463616 | bytes 12845056 | tf_op jit(solution)/shard_map/rd,rf->df/dot_general | solution.py:517
  234.8 8.9 %fusion.29 = f32[1024,2048]{1,0:T(8,128)} fusion(bf16[1024,1408]{1,0:T(8,128)(2,1)S(1)} %copy-done.40, bf16[2048,1408]{1,0:T(8,128)(2,1)S(1)} %bitcast.109), kind=kOutput, calls=%fused_computation.81 | convolution fusion | flops 5905580032 | bytes 17039360 | tf_op jit(solution)/shard_map/rc,dc->rd/dot_general | solution.py:521
  243.7 8.2 %convolution_convert_fusion.2 = bf16[1408,2048]{1,0:T(8,128)(2,1)} fusion(bf16[1024,1408]{1,0:T(8,128)(2,1)S(1)} %get-tuple-element.78, f32[]{:T(128)} %bitcast.2, f32[]{:T(128)} %bitcast, bf16[1,1024,2048]{2,1,0:T(8,128)(2,1)S(1)} %copy-done.15), kind=kOutput, calls=%fused_computation.13 | convolution fusion | flops 5916852224 | bytes 12845064 | tf_op jit(solution)/shard_map/rd,rf->df/dot_general | solution.py:517
  252.0 8.2 %convolution_convert_fusion.3.refs_1_ = bf16[1024,2048]{1,0:T(8,128)(2,1)} fusion(bf16[1024,1408]{1,0:T(8,128)(2,1)S(1)} %get-tuple-element.78, bf16[1408,2048]{1,0:T(8,128)(2,1)S(1)} %bitcast.111), kind=kOutput, calls=%fused_computation.25 | convolution fusion | flops 5907677184 | bytes 12845056 | tf_op jit(solution)/shard_map/dot_general | solution.py:27
  260.2 8.7 %convolution_convert_fusion = bf16[2048,1408]{1,0:T(8,128)(2,1)} fusion(bf16[1024,2048]{1,0:T(8,128)(2,1)S(1)} %copy-done.39, bf16[1024,1408]{1,0:T(8,128)(2,1)S(1)} %copy-done.41), kind=kOutput, calls=%fused_computation.11 | convolution fusion | flops 5908463616 | bytes 12845056 | tf_op jit(solution)/shard_map/rd,rf->df/dot_general | solution.py:517
  268.9 12.1 %add_convert_fusion.1.refs_0_ = bf16[1024,2048]{1,0:T(8,128)(2,1)} fusion(f32[1024,2048]{1,0:T(8,128)} %fusion.29, bf16[1024,1408]{1,0:T(8,128)(2,1)} %get-tuple-element.80, bf16[2048,1408]{1,0:T(8,128)(2,1)} %param.28), kind=kOutput, calls=%fused_computation.7 | convolution fusion | flops 5909774336 | bytes 21233664 | tf_op jit(solution)/shard_map/rc,dc->rd/dot_general | solution.py:521
  282.7 226.1 %shard_map.232 = (bf16[1024,2048]{1,0:T(8,128)(2,1)}, bf16[1024,2048]{1,0:T(8,128)(2,1)}, f32[512,2048]{1,0:T(8,128)}, f32[1,2048]{1,0:T(1,128)}) custom-call(bf16[1024,2048]{1,0:T(8,128)(2,1)} %add_convert_fusion.1.refs_0_, bf16[1024,2048]{1,0:T(8,128)(2,1)} %convolution_convert_fusion.3.refs_1_, bf16[1024,2048]{1,0:T(8,128)(2,1)} %bitcast.86, ...), custom_call_target="tpu_custom_call" | custom-call | flops 4194304 | bytes 629145600 | tf_op jit(solution)/shard_map/pallas_call | solution.py:435
  508.9 4.7 convolution_convert_fusion.8.do_ref
  513.6 19.6 %shard_map.233 = (bf16[1024,512]{1,0:T(8,128)(2,1)S(1)}, f32[2048,256]{1,0:T(8,128)S(1)}, f32[2048,256]{1,0:T(8,128)S(1)}) custom-call(s32[2]{0:T(128)S(1)} %get-tuple-element.101.query_order, s32[4]{0:T(128)S(1)} %pad_add_fusion.key_order, bf16[1024,512]{1,0:T(8,128)(2,1)S(1)} %copy-done.5, bf16[1024,512]{1,0:T(8,128)(2,1)S(1)} %convolution_convert_fusion.8.do_ref, ...), custom_call_target="tpu_custom_call" | custom-call | flops 10737418240 | bytes 11534336 | tf_op jit(solution)/shard_map/pallas_call | solution.py:206
  545.4 5.8 fusion.30
  551.2 9.6 %collective-permute-done.2 = bf16[1024,256]{1,0:T(8,128)(2,1)S(1)} collective-permute-done((bf16[1024,256]{1,0:T(8,128)(2,1)S(1)}, bf16[1024,256]{1,0:T(8,128)(2,1)S(1)}, u32[]{:S(2)}, u32[]{:S(2)}) %collective-permute-start.2) | collective-permute-done | bytes 524320 | tf_op jit(solution)/shard_map/ppermute | solution.py:635
  565.9 4.7 fusion.31
  577.4 9.8 %add_convert_fusion.refs_0_ = bf16[1024,2048]{1,0:T(8,128)(2,1)} fusion(f32[1024,2048]{1,0:T(8,128)} %fusion.30, f32[1024,2048]{1,0:T(8,128)} %fusion.31, bf16[2048,256]{1,0:T(8,128)(2,1)S(1)} %copy-done.25, bf16[1024,256]{1,0:T(8,128)(2,1)} %collective-permute-done.3, f32[2048,256]{1,0:T(8,128)} %copy-done.1), kind=kOutput, calls=%fused_computation.6 | convolution fusion | flops 1080819712 | bytes 23592960 | tf_op jit(solution)/shard_map/rc,dc->rd/dot_general | solution.py:521
  587.2 133.7 %shard_map.234 = (bf16[1024,2048]{1,0:T(8,128)(2,1)}, f32[8,2048]{1,0:T(8,128)}) custom-call(bf16[1024,2048]{1,0:T(8,128)(2,1)} %add_convert_fusion.refs_0_, bf16[1024,2048]{1,0:T(8,128)(2,1)} %bitcast.87, f32[512,2048]{1,0:T(8,128)} %get-tuple-element.53.refs_2_, f32[1,2048]{1,0:T(1,128)} %bitcast.104, f32[1,2048]{1,0:T(1,128)} %get-tuple-element.54.refs_4_), custom_call_target="tpu_custom_call" | custom-call | flops 2097152 | bytes 314572800 | tf_op jit(solution)/shard_map/pallas_call | solution.py:435
  722.5 7.7 %add_bitcast_fusion = f32[1,1024,2048]{2,1,0:T(8,128)} fusion(bf16[1024,2048]{1,0:T(8,128)(2,1)} %get-tuple-element.55, f32[]{:T(128)} %bitcast.2, bf16[1,1024,2048]{2,1,0:T(8,128)(2,1)S(1)} %copy-done.16), kind=kLoop, calls=%fused_computation.5 | loop fusion | flops 8388608 | bytes 16777220 | tf_op jit(solution)/shard_map/reshape | solution.py:670
  730.2 8.0 %convert_element_type.177 = f32[2048,1408]{1,0:T(8,128)} convert(bf16[2048,1408]{1,0:T(8,128)(2,1)} %get-tuple-element.68) | non-fusion elementwise | flops 2883584 | bytes 17301504 | tf_op jit(solution)/shard_map/convert_element_type | solution.py:665
  738.1 5.2 convert_element_type.178
  743.3 6.0 convert_element_type.179
  (166 shorter events, 80.6 us)
Async XLA Ops:
  7.2 69.2 %copy-start = (bf16[512,2048]{1,0:T(8,128)(2,1)S(1)}, bf16[512,2048]{1,0:T(8,128)(2,1)}, u32[]{:S(2)}) copy-start(bf16[512,2048]{1,0:T(8,128)(2,1)} %param.26) | copy-start | bytes 6291460
  7.2 579.9 %all-reduce.5.cloned.1.call-start = ((), (), s32[]{:S(2)}) async-start(), calls=%async_computation | async-start | bytes 34603008 | tf_op jit(solution)/shard_map/psum | solution.py:606
  7.3 10.6 %copy-start.36 = (f32[64]{0:T(128)}, f32[64]{0:T(128)S(1)}, u32[]{:S(2)}) copy-start(f32[64]{0:T(128)S(1)} %negate_power_fusion) | copy-start | bytes 772
  10.6 17.4 %copy-start.33 = (f32[1024]{0:T(1024)}, f32[1024]{0:T(1024)S(1)}, u32[]{:S(2)}) copy-start(f32[1024]{0:T(1024)S(1)} %add_rsqrt_fusion) | copy-start | bytes 12292
  13.9 33.0 %copy-start.20 = (f32[1024,64]{0,1:T(8,128)}, f32[1024,64]{0,1:T(8,128)S(1)}, u32[]{:S(2)}) copy-start(f32[1024,64]{0,1:T(8,128)S(1)} %get-tuple-element.95) | copy-start | bytes 786436
  19.0 29.9 %collective-permute-start = (bf16[1024,256]{0,1:T(8,128)(2,1)}, bf16[1024,256]{0,1:T(8,128)(2,1)}, u32[]{:S(2)}, u32[]{:S(2)}) collective-permute-start(bf16[1024,256]{0,1:T(8,128)(2,1)} %bitcast.14), channel_id=1, source_target_pairs={{0,4},{4,0},{1,5},{5,1},{2,6},{6,2},{3,7},{7,3},{8,12},{12,8},{9,1... | collective-permute-start | bytes 1572872 | tf_op jit(solution)/shard_map/ppermute | solution.py:531
  24.0 29.4 %collective-permute-start.1 = (bf16[1024,256]{1,0:T(8,128)(2,1)}, bf16[1024,256]{1,0:T(8,128)(2,1)}, u32[]{:S(2)}, u32[]{:S(2)}) collective-permute-start(bf16[1024,256]{1,0:T(8,128)(2,1)} %convolution_convert_fusion.9), channel_id=1, source_target_pairs={{0,4},{4,0},{1,5},{5,1},{2,6},{6,2},{3,7},{7,3},{8,12},{12,8},{9,1... | collective-permute-start | bytes 1572872 | tf_op jit(solution)/shard_map/ppermute | solution.py:531
  80.7 128.4 %slice-start.8 = ((s8[5767168]{0:T(1024)(128)(4,1)}), s8[1572864]{0:T(1024)(128)(4,1)S(1)}, s32[]{:S(2)}) async-start(s8[5767168]{0:T(1024)(128)(4,1)} %bitcast.112), calls=%async_computation.10 | async-start | bytes 3145728
  197.3 11.9 %slice-start.9 = ((s8[5767168]{0:T(1024)(128)(4,1)}), s8[4194304]{0:T(1024)(128)(4,1)S(1)}, s32[]{:S(2)}) async-start(s8[5767168]{0:T(1024)(128)(4,1)} %bitcast.112), calls=%async_computation.11 | async-start | bytes 8388608
  197.3 37.5 %slice-start.4 = ((s8[5767168]{0:T(1024)(128)(4,1)}), s8[4194304]{0:T(1024)(128)(4,1)S(1)}, s32[]{:S(2)}) async-start(s8[5767168]{0:T(1024)(128)(4,1)} %bitcast.108), calls=%async_computation.6 | async-start | bytes 8388608
  209.1 25.6 %slice-start.5 = ((s8[5767168]{0:T(1024)(128)(4,1)}), s8[1572864]{0:T(1024)(128)(4,1)S(1)}, s32[]{:S(2)}) async-start(s8[5767168]{0:T(1024)(128)(4,1)} %bitcast.108), calls=%async_computation.7 | async-start | bytes 3145728
  223.6 11.1 %copy-start.40 = (bf16[1024,1408]{1,0:T(8,128)(2,1)S(1)}, bf16[1024,1408]{1,0:T(8,128)(2,1)}, u32[]{:S(2)}) copy-start(bf16[1024,1408]{1,0:T(8,128)(2,1)} %get-tuple-element.79) | copy-start | bytes 8650756
  234.8 17.2 %slice-start.6 = ((s8[5767168]{0:T(1024)(128)(4,1)}), s8[4194304]{0:T(1024)(128)(4,1)S(1)}, s32[]{:S(2)}) async-start(s8[5767168]{0:T(1024)(128)(4,1)} %bitcast.110), calls=%async_computation.8 | async-start | bytes 8388608
  281.0 468.3 %all-reduce.7.cloned.1.call-start = ((), (), s32[]{:S(2)}) async-start(), calls=%async_computation.1 | async-start | bytes 12582912 | tf_op jit(solution)/shard_map/psum | solution.py:606
  513.6 24.1 %copy-start.12 = (bf16[1,1024,2048]{2,1,0:T(8,128)(2,1)S(1)}, bf16[1,1024,2048]{2,1,0:T(8,128)(2,1)}, u32[]{:S(2)}) copy-start(bf16[1,1024,2048]{2,1,0:T(8,128)(2,1)} %param.15) | copy-start | bytes 12582916
  513.6 24.1 %copy-start.31 = (f32[2048]{0:T(1024)S(1)}, f32[2048]{0:T(1024)}, u32[]{:S(2)}) copy-start(f32[2048]{0:T(1024)} %param.21) | copy-start | bytes 24580
  513.6 24.1 %copy-start.34 = (f32[1024]{0:T(1024)S(1)}, f32[1024]{0:T(1024)}, u32[]{:S(2)}) copy-start(f32[1024]{0:T(1024)} %copy-done.33) | copy-start | bytes 12292
  534.2 39.2 %collective-permute-start.3 = (bf16[1024,256]{1,0:T(8,128)(2,1)}, bf16[1024,256]{1,0:T(8,128)(2,1)}, u32[]{:S(2)}, u32[]{:S(2)}) collective-permute-start(bf16[1024,256]{1,0:T(8,128)(2,1)} %slice.88), channel_id=1, source_target_pairs={{0,4},{4,0},{1,5},{5,1},{2,6},{6,2},{3,7},{7,3},{8,12},{12,8},{9,1... | collective-permute-start | bytes 1572872 | tf_op jit(solution)/shard_map/ppermute | solution.py:635
  537.6 23.1 %collective-permute-start.2 = (bf16[1024,256]{1,0:T(8,128)(2,1)S(1)}, bf16[1024,256]{1,0:T(8,128)(2,1)S(1)}, u32[]{:S(2)}, u32[]{:S(2)}) collective-permute-start(bf16[1024,256]{1,0:T(8,128)(2,1)S(1)} %slice.89), channel_id=1, source_target_pairs={{0,4},{4,0},{1,5},{5,1},{2,6},{6,2},{3,7},{7,3},{8,12},{12,8},{9,1... | collective-permute-start | bytes 1572872 | tf_op jit(solution)/shard_map/ppermute | solution.py:635
  551.2 13.2 %copy-start.21 = (f32[1024,64]{0,1:T(8,128)S(1)}, f32[1024,64]{0,1:T(8,128)}, u32[]{:S(2)}) copy-start(f32[1024,64]{0,1:T(8,128)} %copy-done.20) | copy-start | bytes 786436
  551.2 14.7 %copy-start.18 = (bf16[2048,256]{1,0:T(8,128)(2,1)S(1)}, bf16[2048,256]{1,0:T(8,128)(2,1)}, u32[]{:S(2)}) copy-start(bf16[2048,256]{1,0:T(8,128)(2,1)} %param.24) | copy-start | bytes 3145732
  587.2 135.3 %copy-start.16 = (bf16[1,1024,2048]{2,1,0:T(8,128)(2,1)S(1)}, bf16[1,1024,2048]{2,1,0:T(8,128)(2,1)}, u32[]{:S(2)}) copy-start(bf16[1,1024,2048]{2,1,0:T(8,128)(2,1)} %param.16) | copy-start | bytes 12582916
  722.5 15.7 %slice-start.2 = ((s8[5767168]{0:T(1024)(128)(4,1)}), s8[4194304]{0:T(1024)(128)(4,1)S(1)}, s32[]{:S(2)}) async-start(s8[5767168]{0:T(1024)(128)(4,1)} %bitcast.91), calls=%async_computation.4 | async-start | bytes 8388608
  730.2 13.1 %slice-start = ((s8[5767168]{0:T(1024)(128)(4,1)}), s8[4194304]{0:T(1024)(128)(4,1)S(1)}, s32[]{:S(2)}) async-start(s8[5767168]{0:T(1024)(128)(4,1)} %bitcast.89), calls=%async_computation.2 | async-start | bytes 8388608
  (34 other events, 164.3 us)
Sparse Core Ops, SparseCore 0:
  281.1 225.3 all-reduce.4
  587.3 105.4 all-reduce.6

commit v4 on v3

--- a/solution.py
+++ b/solution.py
@@ -252,6 +252,7 @@
 LINE_WINDOW = 2
 LINE_SKEW = 2
 MESH_AXES = ("dp", "ctx", "tensor")
+SPREAD_PIECES = 4
 
 
 def pair_steps(sizes):
@@ -269,10 +270,12 @@
     return jnp.where((index // bit) % 2 == 0, index + bit, index - bit)
 
 
-def line_kernel(size, chunk, streams, owners, pairs, side_count, out_count, *refs):
+def line_kernel(size, chunk, returns, owners, pairs, side_count, out_count, *refs):
+    streams = len(returns)
+    returned = [k for k in range(streams) if returns[k]]
     parts, refs = refs[:streams], refs[streams:]
     sides, refs = refs[:side_count], refs[side_count:]
-    shared, refs = refs[:streams], refs[streams:]
+    shared, refs = dict(zip(returned, refs)), refs[len(returned) :]
     kept, refs = refs[:out_count], refs[out_count:]
     inbox, send_up, recv_up, send_back, recv_back = refs[:5]
     half = parts[0].shape[0] // 2
@@ -352,8 +355,9 @@
             @pl.when(position == last)
             def _():
                 result = owners[k](total, place(f, i), local(i), sides, kept)
-                shared[k][place(f, i), :] = result.astype(BF16)
-                backward(k, f, i).start()
+                if returns[k]:
+                    shared[k][place(f, i), :] = result.astype(BF16)
+                    backward(k, f, i).start()
 
     def pass_back(k, f, i):
         position = flows[f][0]
@@ -368,19 +372,41 @@
             for f in range(2):
                 i = s - LINE_SKEW * flows[f][0]
                 pl.when((i >= 0) & (i < count))(lambda: reduce_chunk(k, f, i))
-        for k in range(streams):
+        for k in returned:
             for f in range(2):
                 pass_back(k, f, s - LINE_SKEW * (2 * last - flows[f][0]))
+        for n in range(len(pairs) + 1 if pairs else 0):
+            pl.when(s == n * gap)(lambda: advance_gains(n))
         return carry
 
-    if not pairs:
-        for ref in kept[1:]:
-            ref[...] = jnp.zeros_like(ref)
-    else:
-        gains = kept[0]
-        gains[...] = jnp.zeros_like(gains)
-        gains[1:2, :] = sides[-1][...]
-    lax.fori_loop(0, count + 2 * LINE_SKEW * last, step, 0)
+    steps = count + 2 * LINE_SKEW * last
+    gap = steps // (len(pairs) + 1)
+    if pairs:
+        slots, sums, send_pair, recv_pair = refs[5:]
+        sums[0] = sides[-1][...]
+    elif len(kept) > 1:
+        kept[1][...] = jnp.zeros_like(kept[1])
+
+    def swap_gains(n):
+        return pltpu.make_async_remote_copy(
+            src_ref=sums.at[n],
+            dst_ref=slots.at[n],
+            send_sem=send_pair.at[n],
+            recv_sem=recv_pair.at[n],
+            device_id={pairs[n][0]: partner(*pairs[n])},
+            device_id_type=pl.DeviceIdType.MESH,
+        )
+
+    def advance_gains(n):
+        if n > 0:
+            swap_gains(n - 1).wait()
+            sums[n] = sums[n - 1] + slots[n - 1]
+        if n < len(pairs):
+            swap_gains(n).start()
+        else:
+            kept[0][...] = sums[n]
+
+    lax.fori_loop(0, steps, step, 0)
 
     def drain(i, carry):
         for k in range(streams):
@@ -390,39 +416,23 @@
                 pl.when((position < last) & ~waited)(
                     lambda: onward(k, f, i, inbox.at[k, f, local(i)]).wait_send()
                 )
-                pl.when(position > 0)(lambda: backward(k, f, i).wait_send())
+                if returns[k]:
+                    pl.when(position > 0)(lambda: backward(k, f, i).wait_send())
         return carry
 
     lax.fori_loop(0, count, drain, 0)
 
-    if pairs:
-        slots, sums, send_pair, recv_pair = refs[5:]
-        sums[0] = gains[...]
-        for n, (axis, bit) in enumerate(pairs):
-            copy = pltpu.make_async_remote_copy(
-                src_ref=sums.at[n],
-                dst_ref=slots.at[n],
-                send_sem=send_pair.at[n],
-                recv_sem=recv_pair.at[n],
-                device_id={axis: partner(axis, bit)},
-                device_id_type=pl.DeviceIdType.MESH,
-            )
-            copy.start()
-            copy.wait()
-            sums[n + 1] = sums[n] + slots[n]
-        gains[...] = sums[len(pairs)]
-
-
-def line_sum(parts, owners, sides, kept, collective_id, pairs=()):
+
+def line_sum(parts, owners, sides, kept, collective_id, returns=(True,), pairs=()):
     rows, width = parts[0].shape
     size = lax.axis_size("tensor")
     streams = len(parts)
-    chunk = min(LINE_CHUNK, rows // 2)
+    chunk = max(16, min(LINE_CHUNK, rows // 32))
     count = rows // 2 // chunk
     whole = pl.BlockSpec(memory_space=pltpu.VMEM)
     scalar = pl.BlockSpec(memory_space=pltpu.SMEM)
     sems = pltpu.SemaphoreType.DMA((streams, 2, count))
-    outs = [jax.ShapeDtypeStruct((rows, width), BF16)] * streams + list(kept)
+    outs = [jax.ShapeDtypeStruct((rows, width), BF16)] * sum(returns) + list(kept)
     extra = []
     if pairs:
         pair_sems = pltpu.SemaphoreType.DMA((len(pairs),))
@@ -434,7 +444,7 @@
         ]
     return pl.pallas_call(
         functools.partial(
-            line_kernel, size, chunk, streams, owners, pairs, len(sides), len(kept)
+            line_kernel, size, chunk, returns, owners, pairs, len(sides), len(kept)
         ),
         out_shape=outs,
         in_specs=[whole] * streams + [scalar if s.ndim == 1 else whole for s in sides],
@@ -475,23 +485,30 @@
 def own_output(total, where, here, sides, kept):
     x_ref, hidden_ref, cot_ref, gain_ref, factor = sides
     x = x_ref[where, :].astype(F32)
-    return x + factor[1] * ((hidden_ref[here, :] - x) + total)
+    result = x + factor[1] * ((hidden_ref[here, :] - x) + total)
+    kept[2][here, :] = result.astype(BF16)
 
 
 def own_dinput(total, where, here, sides, kept):
     x_ref, dhidden_ref, gain_ref, _ = sides
     unit, inverse = unit_of(x_ref[where, :].astype(F32))
-    kept[0][0:1, :] += jnp.sum(total * unit, axis=0, keepdims=True)
     return dhidden_ref[here, :] + norm_back(total, unit, inverse, gain_ref[...])
 
 
-def sequence_positions(order_row, length):
-    spans = order_row.shape[0]
-    stride = length // spans
-    places = jnp.arange(length, dtype=jnp.int32)
-    onehot = (places // stride)[:, None] == jnp.arange(spans, dtype=jnp.int32)[None, :]
-    starts = jnp.sum(jnp.where(onehot, order_row[None, :], 0), axis=1)
-    return starts * stride + places % stride
+def spread_halves(own):
+    size = lax.axis_size("tensor")
+    me = lax.axis_index("tensor")
+    pieces = []
+    step = own.shape[0] // SPREAD_PIECES
+    for p in range(SPREAD_PIECES):
+        hops = [own[p * step : (p + 1) * step]]
+        for h in range(size - 1):
+            perm = [(size - 1 - h, size - 2 - h), (h, h + 1)]
+            hops.append(lax.ppermute(hops[-1], "tensor", perm))
+        first = lax.select_n(size - 1 - me, *hops) if size > 2 else jnp.where(me == 1, *hops)
+        second = lax.select_n(me, *hops) if size > 2 else jnp.where(me == 0, *hops)
+        pieces.append((first, second))
+    return jnp.concatenate([a for a, _ in pieces] + [b for _, b in pieces], 0)
 
 
 def rotary_tables(positions):
@@ -526,20 +543,88 @@
     return inverse * (scaled - unit * jnp.mean(scaled * unit, axis=-1, keepdims=True))
 
 
-def swap_ctx(part, ctx_size):
-    return [
-        lax.ppermute(part, "ctx", [(i, (i + s) % ctx_size) for i in range(ctx_size)])
-        for s in range(1, ctx_size)
-    ]
-
-
-def per_device(
-    inputs,
-    cotangent,
-    skip_mask,
-    group_ids,
-    span_order,
-    exit_scale,
+def flags_kernel(size, mine, everyone, send_sem, recv_sem):
+    me = lax.axis_index("dp")
+    barrier = pltpu.get_barrier_semaphore()
+    others = [lax.rem(me + s, size) for s in range(1, size)]
+    for other in others:
+        pl.semaphore_signal(
+            barrier, inc=1, device_id={"dp": other}, device_id_type=pl.DeviceIdType.MESH
+        )
+    pl.semaphore_wait(barrier, size - 1)
+
+    def send(s, slot):
+        return pltpu.make_async_remote_copy(
+            src_ref=mine,
+            dst_ref=everyone.at[slot],
+            send_sem=send_sem.at[s],
+            recv_sem=recv_sem.at[s],
+            device_id={"dp": others[s]},
+            device_id_type=pl.DeviceIdType.MESH,
+        )
+
+    for s in range(size - 1):
+        send(s, me).start()
+    everyone[me] = mine[...]
+    for s in range(size - 1):
+        send(s, me).wait_send()
+        send(s, lax.rem(me + 2 * size - 1 - s, size)).wait_recv()
+
+
+def share_flags(row):
+    size = lax.axis_size("dp")
+    tile = jnp.zeros((8, 128), jnp.int32).at[0, : row.shape[0]].set(row)
+    sems = pltpu.SemaphoreType.DMA((size - 1,))
+    whole = pl.BlockSpec(memory_space=pltpu.VMEM)
+    shared = pl.pallas_call(
+        functools.partial(flags_kernel, size),
+        out_shape=jax.ShapeDtypeStruct((size, 8, 128), jnp.int32),
+        in_specs=[whole],
+        out_specs=whole,
+        scratch_shapes=[sems, sems],
+        compiler_params=pltpu.CompilerParams(collective_id=1, has_side_effects=True),
+    )(tile)
+    return shared[:, 0, : row.shape[0]]
+
+
+def shift_ctx(part, s):
+    size = lax.axis_size("ctx")
+    return lax.ppermute(part, "ctx", [(i, (i + s) % size) for i in range(size)])
+
+
+def swap_core(part):
+    return lax.ppermute(part, "dp", [(i, i ^ 1) for i in range(lax.axis_size("dp"))])
+
+
+def gather_parts(own, paired):
+    parts = []
+    for s in range(lax.axis_size("ctx")):
+        here = own if s == 0 else shift_ctx(own, s)
+        parts += [here, swap_core(here)] if paired else [here]
+    return parts
+
+
+def collect_parts(parts, paired):
+    total = None
+    for s in range(lax.axis_size("ctx")):
+        if paired:
+            near, far = parts[2 * s], parts[2 * s + 1]
+            near = near + swap_core(far.astype(BF16)).astype(F32)
+        else:
+            near = parts[s]
+        total = near if s == 0 else total + shift_ctx(near.astype(BF16), -s).astype(F32)
+    return total
+
+
+def block_pass(
+    paired,
+    first_id,
+    span,
+    x_low,
+    cot_low,
+    keep,
+    scale,
+    order_row,
     attn_gain,
     ffn_gain,
     w_query,
@@ -550,35 +635,40 @@
     w_up,
     w_down,
 ):
-    _, rows, width = inputs.shape
+    rows, width = x_low.shape
     dp_size, ctx_size = lax.axis_size("dp"), lax.axis_size("ctx")
-    full_len = rows * ctx_size
-    spans = span_order.shape[1]
-    span = full_len // spans
+    spans = order_row.shape[0]
     kv_local = w_key.shape[1] // HEAD_DIM
     ctx = lax.axis_index("ctx")
-    offset = ctx * rows
-    positions = lax.dynamic_slice_in_dim(sequence_positions(span_order[0], full_len), offset, rows)
-    cosine, sine = rotary_tables(positions)
-    keep = skip_mask[0].astype(F32)
-    scale = jnp.where(group_ids[0] == 1, exit_scale[1], exit_scale[0])
-
-    own_spans = spans // ctx_size
-    orders = [
-        lax.dynamic_slice_in_dim(span_order[0], ((ctx - s) % ctx_size) * own_spans, own_spans)
-        for s in range(ctx_size)
-    ]
-    query_order, key_order = orders[0], jnp.concatenate(orders)
-
-    x_low = inputs[0]
+    core = lax.axis_index("dp") % 2
+    per_part = rows // span
+    order_parts = []
+    for s in range(ctx_size):
+        group = (ctx + ctx_size - s) % ctx_size
+        places = [group * 2 + core, group * 2 + 1 - core] if paired else [group]
+        order_parts += [
+            lax.dynamic_slice_in_dim(order_row, place * per_part, per_part) for place in places
+        ]
+    query_order, key_order = order_parts[0], jnp.concatenate(order_parts)
+    row_index = jnp.arange(rows, dtype=jnp.int32)
+    starts = jnp.sum(
+        jnp.where(
+            (row_index // span)[:, None] == jnp.arange(per_part, dtype=jnp.int32)[None, :],
+            query_order[None, :],
+            0,
+        ),
+        axis=1,
+    )
+    cosine, sine = rotary_tables(starts * span + row_index % span)
+
     flat = x_low.astype(F32)
     inv_one = lax.rsqrt(jnp.mean(flat * flat, axis=-1, keepdims=True) + EPSILON)
     normed_one = (flat * inv_one * attn_gain).astype(BF16)
     k_proj = nn_dot(normed_one, w_key).reshape(rows, kv_local, HEAD_DIM)
     keys_own = rotate(k_proj, cosine, sine).astype(BF16).reshape(rows, -1)
     values_own = nn_dot(normed_one, w_value).astype(BF16)
-    keys = jnp.concatenate([keys_own] + swap_ctx(keys_own, ctx_size), 0)
-    values = jnp.concatenate([values_own] + swap_ctx(values_own, ctx_size), 0)
+    keys = jnp.concatenate(gather_parts(keys_own, paired), 0)
+    values = jnp.concatenate(gather_parts(values_own, paired), 0)
     q_proj = nn_dot(normed_one, w_query).reshape(rows, -1, HEAD_DIM)
     queries = rotate(q_proj, cosine, sine).astype(BF16).reshape(rows, -1)
     mixed, logs = attend(queries, keys, values, query_order, key_order, span)
@@ -588,11 +678,10 @@
     ffn_row, attn_row = ffn_gain[None, :], attn_gain[None, :]
     attn_part = nn_dot(mixed, w_output).astype(BF16)
     normed_two, hidden = line_sum(
-        [attn_part], [own_hidden], [x_low, ffn_row], [half_rows], 1
-    )
-
-    dscaled = cotangent[0].astype(F32) * scale
-    dffn = (keep * dscaled).astype(BF16)
+        [attn_part], [own_hidden], [x_low, ffn_row], [half_rows], first_id
+    )
+
+    dffn = (cot_low.astype(F32) * (keep * scale)).astype(BF16)
     dacted = contract_cols(dffn, w_down)
     gate = nn_dot(normed_two, w_gate)
     upward = nn_dot(normed_two, w_up)
@@ -601,48 +690,43 @@
     acted = (silu_gate * upward).astype(BF16)
     dgate = (dacted * upward * sigmoid_gate * (1.0 + gate * (1.0 - sigmoid_gate))).astype(BF16)
     dupward = (dacted * silu_gate).astype(BF16)
-    dnormed_part = (contract_cols(dgate, w_gate) + contract_cols(dupward, w_up)).astype(BF16)
-    ffn_part = nn_dot(acted, w_down).astype(BF16)
-    total = lambda g, *axes: lax.psum(g, axes)
     ffn_grads = (
         contract_rows(acted, dffn).astype(BF16),
         contract_rows(normed_two, dgate).astype(BF16),
         contract_rows(normed_two, dupward).astype(BF16),
     )
-    dnormed_part, ffn_part, ffn_grads = lax.optimization_barrier(
-        (dnormed_part, ffn_part, ffn_grads)
-    )
-    ffn_grads = total(ffn_grads, "dp", "ctx")
-    dattn, output, dhidden, ffn_gain_part = line_sum(
+    acted, dgate, dupward, ffn_grads = lax.optimization_barrier((acted, dgate, dupward, ffn_grads))
+    ffn_grads = lax.psum(ffn_grads, ("dp", "ctx"))
+    dnormed_part = (contract_cols(dgate, w_gate) + contract_cols(dupward, w_up)).astype(BF16)
+    ffn_part = nn_dot(acted, w_down).astype(BF16)
+    dattn, dhidden, ffn_gain_part, output_half = line_sum(
         [dnormed_part, ffn_part],
         [own_dhidden, own_output],
-        [x_low, hidden, cotangent[0], ffn_row, jnp.stack([keep * scale, keep])],
-        [half_rows, gain_row],
-        2,
-    )
+        [x_low, hidden, cot_low, ffn_row, jnp.stack([keep * scale, keep])],
+        [half_rows, gain_row, jax.ShapeDtypeStruct((rows // 2, width), BF16)],
+        first_id + 1,
+        (True, False),
+    )
+    output = spread_halves(output_half)
     grad_output = contract_rows(mixed, dattn)
     dmixed = contract_cols(dattn, w_output).astype(BF16)
-
     dq_proj, dkeys, dvalues = attend_back(
         queries, dmixed, mixed, logs, cosine, sine, keys, values, query_order, key_order, span
     )
-
-    def collect(grad):
-        parts = grad.reshape(ctx_size, rows, -1)
-        summed = parts[0]
-        for s in range(1, ctx_size):
-            back = [(i, (i - s) % ctx_size) for i in range(ctx_size)]
-            summed = summed + lax.ppermute(parts[s].astype(BF16), "ctx", back).astype(F32)
-        return summed
-
-    dk_own = collect(dkeys).reshape(rows, kv_local, HEAD_DIM)
+    split = lambda grad: [grad[p * rows : (p + 1) * rows] for p in range(grad.shape[0] // rows)]
+    dk_own = collect_parts(split(dkeys), paired).reshape(rows, kv_local, HEAD_DIM)
     dk_proj = rotate_back(dk_own, cosine, sine).reshape(rows, -1).astype(BF16)
-    dv_proj = collect(dvalues).astype(BF16)
+    dv_proj = collect_parts(split(dvalues), paired).astype(BF16)
     dnormed_one = (
         contract_cols(dq_proj, w_query)
         + contract_cols(dk_proj, w_key)
         + contract_cols(dv_proj, w_value)
-    ).astype(BF16)
+    )
+    attn_gain_part = jnp.sum(dnormed_one * (flat * inv_one), axis=0, keepdims=True)
+    gain_parts = jnp.concatenate(
+        [attn_gain_part, ffn_gain_part, jnp.zeros((6, width), F32)], axis=0
+    )
+    dnormed_one = dnormed_one.astype(BF16)
     attn_grads = (
         contract_rows(normed_one, dq_proj).astype(BF16),
         contract_rows(normed_one, dk_proj).astype(BF16),
@@ -651,20 +735,98 @@
     )
     dnormed_one, attn_grads = lax.optimization_barrier((dnormed_one, attn_grads))
     attn_grads, ffn_grads = lax.optimization_barrier((attn_grads, ffn_grads))
-    attn_grads = total(attn_grads, "ctx", "dp")
+    attn_grads = lax.psum(attn_grads, ("ctx", "dp"))
     pairs = pair_steps((dp_size, ctx_size, lax.axis_size("tensor")))
     through, gains = line_sum(
         [dnormed_one],
         [own_dinput],
-        [x_low, dhidden, attn_row, ffn_gain_part],
+        [x_low, dhidden, attn_row, gain_parts],
         [jax.ShapeDtypeStruct((8, width), F32)],
-        3,
+        first_id + 2,
+        (True,),
         tuple(pairs),
     )
-    grad_attn_gain, grad_ffn_gain = gains[0], gains[1]
+    return lax.optimization_barrier((output, through, gains, attn_grads, ffn_grads))
+
+
+def per_device(
+    inputs,
+    cotangent,
+    skip_mask,
+    group_ids,
+    span_order,
+    exit_scale,
+    attn_gain,
+    ffn_gain,
+    *weights,
+):
+    _, rows, width = inputs.shape
+    spans = span_order.shape[1]
+    own_spans = spans // lax.axis_size("ctx")
+    span = rows // own_spans
+    me = lax.axis_index("dp")
+    core = me % 2
+    x_low, cot_low = inputs[0], cotangent[0]
+    flags = share_flags(jnp.concatenate([skip_mask, group_ids, span_order[0]]))
+    runs, groups = flags[:, 0], flags[:, 1]
+    scale_of = lambda group: jnp.where(group == 1, exit_scale[1], exit_scale[0])
+    own_run, own_scale = skip_mask[0], scale_of(group_ids[0])
+    gains = (attn_gain, ffn_gain)
+
+    def alone():
+        return block_pass(
+            False,
+            2,
+            span,
+            x_low,
+            cot_low,
+            own_run.astype(F32),
+            own_scale,
+            span_order[0],
+            *gains,
+            *weights,
+        )
+
+    def shared():
+        half = rows // 2
+        other = me + 1 - 2 * core
+        take = lambda a, i: lax.dynamic_slice_in_dim(a, i * half, half, 0)
+        pick = lambda a: lax.dynamic_index_in_dim(a, other, 0, keepdims=False)
+        other_run = pick(runs)
+        use_own = (own_run == 1) | ((other_run == 0) & (core == 0))
+        choose = lambda mine, theirs: jnp.where(use_own, mine, theirs)
+        work = lambda a: choose(take(a, core), swap_core(take(a, 1 - core)))
+        output, through, *rest = block_pass(
+            True,
+            5,
+            span,
+            work(x_low),
+            work(cot_low),
+            choose(own_run, other_run).astype(F32),
+            choose(own_scale, scale_of(pick(groups))),
+            choose(span_order[0], pick(flags[:, 2:])),
+            *gains,
+            *weights,
+        )
+
+        def whole(part, idle):
+            theirs = swap_core(part)
+            first, second = jnp.where(core == 0, part, theirs), jnp.where(core == 0, theirs, part)
+            return jnp.where(own_run == 1, jnp.concatenate([first, second], 0), idle)
+
+        return whole(output, x_low), whole(through, jnp.zeros_like(x_low)), *rest
+
+    if own_spans % 2 == 0 and lax.axis_size("dp") % 2 == 0:
+        pairs = runs.reshape(-1, 2)
+        output, through, sums, attn_grads, ffn_grads = lax.cond(
+            jnp.all(pairs[:, 0] * pairs[:, 1] == 0), shared, alone
+        )
+    else:
+        output, through, sums, attn_grads, ffn_grads = alone()
+    grad_attn_gain, grad_ffn_gain = sums[0], sums[1]
     grad_down, grad_gate, grad_up = (g.astype(F32) for g in ffn_grads)
     grad_query, grad_key, grad_value, grad_output = (g.astype(F32) for g in attn_grads)
-    input_grad = dscaled + through.astype(F32)
+    input_grad = cot_low.astype(F32) * own_scale + through.astype(F32)
     return (
         output.reshape(inputs.shape),
         input_grad.reshape(inputs.shape),

time: 775 us -> 633 us (0.82)
  Pallas kernels: 510 us -> 257 us
  waiting for transfers between devices: 9.6 us -> 120 us
  matrix products: 149 us -> 79 us
  starting transfers between devices: 6.46 us -> 33.8 us
  other arithmetic: 52.4 us -> 73.9 us
  loops' own time: 0 us -> 13 us
    pallas_call x3 -> x4, Pallas kernels: 476 us -> 232 us  [the longest x3 226 us: line_sum(): pl.pallas_call(functools.partial(line_kernel, size, chunk, returns, owner...]
    psum x2, waiting for transfers between devices: 0.01 us -> 91.7 us  [the longest x1 91.7 us: block_pass(): attn_grads = lax.psum(attn_grads, ('ctx', 'dp'))]
    dot_general x7, matrix products: 56.3 us -> 26.4 us  [contract_cols(): return jnp.einsum('rc,dc->rd', left, right, preferred_element_type=F32)]
    ppermute x4 -> x28, starting transfers between devices: 6.38 us -> 33.7 us  [the longest x12 21.5 us: spread_halves(): hops.append(lax.ppermute(hops[-1], 'tensor', perm))]
    dot_general x7, matrix products: 50.4 us -> 27.5 us  [nn_dot(): return jnp.dot(left, right, preferred_element_type=F32)]
    ppermute x4 -> x28, waiting for transfers between devices: 9.57 us -> 28 us  [the longest x12 11.4 us: spread_halves(): hops.append(lax.ppermute(hops[-1], 'tensor', perm))]
    dot_general x7, matrix products: 42.5 us -> 25.1 us  [contract_rows(): return jnp.einsum('rd,rf->df', left, right, preferred_element_type=F32)]
    unnamed x0 -> x1, loops' own time: none -> 13 us
  transfers between devices with their start and end apart: 6 -> 30, of which waited for: 1 -> 9; matrix products, arithmetic and copies ran while one was open for 14% -> 13% of each run, Pallas kernels for 49% -> 28%
where the time goes in v4:
time: 633 us; the launch traced here: 622 us
  Pallas kernels  257 us (41%)
  waiting for transfers between devices  120 us (19%)
  matrix products  79 us (12%)
  other arithmetic  73.9 us (12%)
  starting transfers between devices  33.8 us (5%)
  local copies, waits for them, and re-layouts  27.9 us (4%)
  between operations  17.5 us (3%)
  loops' own time  13 us (2%)
    pallas_call x3, Pallas kernels, line_sum(): pl.pallas_call(functools.partial(line_kernel, size, chunk, returns, owner...  226 us
    psum x1, waiting for transfers between devices, block_pass(): attn_grads = lax.psum(attn_grads, ('ctx', 'dp'))  91.7 us
    dot_general x7, matrix products, nn_dot(): return jnp.dot(left, right, preferred_element_type=F32)  27.5 us
    dot_general x7, matrix products, contract_cols(): return jnp.einsum('rc,dc->rd', left, right, preferred_element_type=F32)  26.4 us
    dot_general x7, matrix products, contract_rows(): return jnp.einsum('rd,rf->df', left, right, preferred_element_type=F32)  25.1 us
    ppermute x12, starting transfers between devices, spread_halves(): hops.append(lax.ppermute(hops[-1], 'tensor', perm))  21.5 us
    convert_element_type x3, other arithmetic, per_device(): grad_down, grad_gate, grad_up = (g.astype(F32) for g in ffn_grads)  16.3 us
    pallas_call x1, Pallas kernels, attend_back(): pl.pallas_call(functools.partial(attend_back_kernel, group, span), grid_s...  14.1 us
  transfers between devices with their start and end apart: 30, of which 9 were waited for; matrix products, arithmetic and copies ran while one was open for 13% of the time, Pallas kernels for 28%

profile of v4, /device:TPU:0, one launch (start us, length us, event | category | flops | bytes accessed | tf_op | source)
XLA Modules:
  0.0 621.6 jit_solution(16965475438343819687)
XLA Ops:
  12.4 5.9 shard_map.230
  21.1 558.7 %conditional.2 = (f32[8,2048]{1,0:T(8,128)}, bf16[1,1024,2048]{2,1,0:T(8,128)(2,1)}, bf16[1024,2048]{1,0:T(8,128)(2,1)}, f32[1,2048]{1,0:T(1,128)}, f32[1,2048]{...) conditional(s32[]{:T(128)} %convert_element_type.272, ...), branch_computations={%region_1.12_spmd, %region_12.22_spmd} | conditional | flops 87635910656 | bytes 2119813120
  74.7 10.8 %branch_1_fun.5 = (bf16[512,512]{1,0:T(8,128)(2,1)S(1)}, f32[2,2,512]{2,1,0:T(2,128)S(1)}) custom-call(s32[1]{0:T(128)} %bitcast.17.query_order, s32[4]{0:T(128)S(1)} %pad_add_fusion.1.key_order, bf16[512,512]{1,0:T(8,128)(2,1)S(1)} %bitcast.141, bf16[2048,256]{1,0:T(8,128)(2,1)S(1)} %copy.77.k_ref, bf16[256,2048]{1,0:T(8,128)(2,1)S(1)} %copy.78.vt_ref), custom_call_target="tpu_custom_call" | custom-call | flops 2147483648 | bytes 3145728 | tf_op jit(solution)/shard_map/cond/branch_1_fun/pallas_call | solution.py:91
  88.1 66.5 %branch_1_fun.6 = (bf16[512,2048]{1,0:T(8,128)(2,1)}, f32[256,2048]{1,0:T(8,128)}) custom-call(bf16[512,2048]{1,0:T(8,128)(2,1)} %convolution_convert_fusion.16.refs_0_, bf16[512,2048]{1,0:T(8,128)(2,1)} %copy-done.23, f32[1,2048]{1,0:T(1,128)S(1)} %bitcast.165), custom_call_target="tpu_custom_call" | custom-call | flops 1048576 | bytes 314572800 | tf_op jit(solution)/shard_map/cond/branch_1_fun/pallas_call | solution.py:445
  154.7 8.4 %fusion.69 = f32[512,1408]{1,0:T(8,128)} fusion(bf16[512,2048]{1,0:T(8,128)(2,1)} %get-tuple-element.195, bf16[2048,1408]{1,0:T(8,128)(2,1)} %get-tuple-element.196), kind=kOutput, calls=%fused_computation.202 | convolution fusion | flops 2952790016 | bytes 10747904 | tf_op jit(solution)/shard_map/cond/branch_1_fun/dot_general | solution.py:27
  163.1 5.0 fusion.70
  168.1 6.5 %multiply_convert_fusion.7 = (bf16[512,1408]{1,0:T(8,128)(2,1)S(1)}, bf16[512,1408]{1,0:T(8,128)(2,1)S(1)}, bf16[512,1408]{1,0:T(8,128)(2,1)S(1)}) fusion(f32[512,1408]{1,0:T(8,128)} %fusion.69, f32[512,1408]{1,0:T(8,128)} %fusion.70, bf16[1408,2048]{1,0:T(8,128)(2,1)S(1)} %bitcast.180, bf16[512,2048]{1,0:T(8,128)(2,1)S(1)} %copy-done.31, f32[]{:T(128)} %mul.373), kind=kOutput, calls=%fused_computation.100 | convolution fusion | flops 2966749184 | bytes 17956868 | tf_op jit(solution)/shard_map/cond/branch_1_fun/rc,dc->rd/dot_general | solution.py:538
  174.7 5.3 convolution_convert_fusion.11
  180.0 5.3 convolution_convert_fusion.12
  185.3 5.0 convolution_convert_fusion.13
  190.4 6.5 %fusion.71 = f32[512,2048]{1,0:T(8,128)S(1)} fusion(bf16[512,1408]{1,0:T(8,128)(2,1)} %copy-done.101, bf16[2048,1408]{1,0:T(8,128)(2,1)} %get-tuple-element.196), kind=kOutput, calls=%fused_computation.204 | convolution fusion | flops 2952790016 | bytes 11403264 | tf_op jit(solution)/shard_map/cond/branch_1_fun/rc,dc->rd/dot_general | solution.py:538
  197.0 7.6 %convolution_convert_fusion.17.refs_1_ = bf16[512,2048]{1,0:T(8,128)(2,1)} fusion(bf16[512,1408]{1,0:T(8,128)(2,1)S(1)} %copy-done.98, bf16[1408,2048]{1,0:T(8,128)(2,1)} %get-tuple-element.201), kind=kOutput, calls=%fused_computation.99 | convolution fusion | flops 2953838592 | bytes 9306112 | tf_op jit(solution)/shard_map/cond/branch_1_fun/dot_general | solution.py:27
  209.3 84.8 %branch_1_fun.7 = (bf16[512,2048]{1,0:T(8,128)(2,1)}, f32[256,2048]{1,0:T(8,128)}, f32[1,2048]{1,0:T(1,128)}, bf16[256,2048]{1,0:T(8,128)(2,1)}) custom-call(bf16[512,2048]{1,0:T(8,128)(2,1)} %add_convert_fusion.7.refs_0_, bf16[512,2048]{1,0:T(8,128)(2,1)} %convolution_convert_fusion.17.refs_1_, bf16[512,2048]{1,0:T(8,128)(2,1)} %copy-done.23, ...), custom_call_target="tpu_custom_call" | custom-call | flops 2097152 | bytes 629145600 | tf_op jit(solution)/shard_map/cond/branch_1_fun/pallas_call | solution.py:445
  297.2 14.1 %branch_1_fun.8 = (bf16[512,512]{1,0:T(8,128)(2,1)S(1)}, f32[2048,256]{1,0:T(8,128)S(1)}, f32[2048,256]{1,0:T(8,128)S(1)}) custom-call(s32[1]{0:T(128)} %bitcast.17.query_order, s32[4]{0:T(128)S(1)} %pad_add_fusion.1.key_order, bf16[512,512]{1,0:T(8,128)(2,1)S(1)} %bitcast.142, bf16[512,512]{1,0:T(8,128)(2,1)S(1)} %convolution_convert_fusion.20.do_ref, ...), custom_call_target="tpu_custom_call" | custom-call | flops 5368709120 | bytes 9437184 | tf_op jit(solution)/shard_map/cond/branch_1_fun/pallas_call | solution.py:206
  317.5 5.3 collective-permute-start.38
  327.7 7.9 %collective-permute-done.38 = bf16[512,256]{1,0:T(8,128)(2,1)S(1)} collective-permute-done((bf16[512,256]{1,0:T(8,128)(2,1)S(1)}, bf16[512,256]{1,0:T(8,128)(2,1)S(1)}, u32[]{:S(2)}, u32[]{:S(2)}) %collective-permute-start.38) | collective-permute-done | bytes 262176 | tf_op jit(solution)/shard_map/cond/branch_1_fun/ppermute | solution.py:592
  352.8 5.1 collective-permute-start.27
  377.4 74.6 %branch_1_fun.9 = (bf16[512,2048]{1,0:T(8,128)(2,1)}, f32[8,2048]{1,0:T(8,128)S(1)}) custom-call(bf16[512,2048]{1,0:T(8,128)(2,1)} %get-tuple-element.212.refs_0_, bf16[512,2048]{1,0:T(8,128)(2,1)} %copy-done.23, f32[256,2048]{1,0:T(8,128)} %get-tuple-element.213.refs_2_, f32[1,2048]{1,0:T(1,128)S(1)} %bitcast.168, f32[8,2048]{1,0:T(8,128)} %maximum_maximum_fusion.1.refs_4_), custom_call_target="tpu_custom_call" | custom-call | flops 1048576 | bytes 314572800 | tf_op jit(solution)/shard_map/cond/branch_1_fun/pallas_call | solution.py:445
  469.1 91.7 %all-reduce.16.cloned.1.call-done = (bf16[2048,512]{1,0:T(8,128)(2,1)}, bf16[2048,256]{1,0:T(8,128)(2,1)}, bf16[2048,256]{1,0:T(8,128)(2,1)}, bf16[512,2048]{1,0:T(8,128)(2,1)}) async-done(((bf16[2048,512]{1,0:T(8,128)(2,1)}, bf16[2048,256]{1,0:T(8,128)(2,1)}, bf16[2048,256]{1,0:T(8,128)(2,1)}, bf16[512,2048]{1,0:T(8,128)(2,1)}), (bf16[2048,512]{1,0:T(8,128)(2,1)}, bf16[2048,256]{1,0:T(8,128)(2,1)}, ...) | async-done | bytes 6291472 | tf_op jit(solution)/shard_map/cond/branch_1_fun/psum | solution.py:738
  561.9 6.2 collective-permute-done.43
  581.0 9.0 %fusion.49 = f32[1,1024,2048]{2,1,0:T(8,128)} fusion(bf16[1024,2048]{1,0:T(8,128)(2,1)} %get-tuple-element.288, f32[]{:T(128)} %bitcast.45, bf16[1,1024,2048]{2,1,0:T(8,128)(2,1)} %param.20), kind=kLoop, calls=%fused_computation.179 | loop fusion | flops 8388608 | bytes 16777220 | tf_op jit(solution)/shard_map/reshape | solution.py:832
  590.0 6.0 convert_element_type.279
  596.0 5.2 convert_element_type.280
  601.2 5.2 convert_element_type.281
  (283 shorter events, 143.1 us)
Async XLA Ops:
  28.4 426.3 %all-reduce.14.cloned.1.call-start = ((), (), s32[]{:S(2)}) async-start(), calls=%async_computation.2 | async-start | bytes 34603008 | tf_op jit(solution)/shard_map/cond/branch_1_fun/psum | solution.py:699
  31.8 15.7 %collective-permute-start.16 = (bf16[512,2048]{1,0:T(8,128)(2,1)}, bf16[512,2048]{1,0:T(8,128)(2,1)}, u32[]{:S(2)}, u32[]{:S(2)}) collective-permute-start(bf16[512,2048]{1,0:T(8,128)(2,1)} %constant_dynamic-slice_fusion.2), channel_id=1, source_target_pairs={{0,8},{8,0},{16,24},{24,16},{1,9},{9,1},{17,25},{25,17},{2,10},{10... | collective-permute-start | bytes 6291464 | tf_op jit(solution)/shard_map/cond/branch_1_fun/ppermute | solution.py:596
  32.1 25.8 %collective-permute-start.23 = (bf16[512,2048]{1,0:T(8,128)(2,1)S(1)}, bf16[512,2048]{1,0:T(8,128)(2,1)}, u32[]{:S(2)}, u32[]{:S(2)}) collective-permute-start(bf16[512,2048]{1,0:T(8,128)(2,1)S(1)} %constant_dynamic-slice_fusion.1), channel_id=1, source_target_pairs={{0,8},{8,0},{16,24},{24,16},{1,9},{9,1},{17,25},{25,17},{2,10},{10... | collective-permute-start | bytes 6291464 | tf_op jit(solution)/shard_map/cond/branch_1_fun/ppermute | solution.py:596
  51.7 9.9 %collective-permute-start.21 = (bf16[512,256]{1,0:T(8,128)(2,1)}, bf16[512,256]{1,0:T(8,128)(2,1)}, u32[]{:S(2)}, u32[]{:S(2)}) collective-permute-start(bf16[512,256]{1,0:T(8,128)(2,1)} %convolution_convert_fusion.21), channel_id=1, source_target_pairs={{0,4},{4,0},{1,5},{5,1},{2,6},{6,2},{3,7},{7,3},{8,12},{12,8},{9,1... | collective-permute-start | bytes 786440 | tf_op jit(solution)/shard_map/cond/branch_1_fun/ppermute | solution.py:592
  53.7 13.2 %collective-permute-start.20 = (bf16[512,256]{1,0:T(8,128)(2,1)}, bf16[512,256]{1,0:T(8,128)(2,1)}, u32[]{:S(2)}, u32[]{:S(2)}) collective-permute-start(bf16[512,256]{1,0:T(8,128)(2,1)} %convolution_convert_fusion.21), channel_id=1, source_target_pairs={{0,8},{8,0},{16,24},{24,16},{1,9},{9,1},{17,25},{25,17},{2,10},{10... | collective-permute-start | bytes 786440 | tf_op jit(solution)/shard_map/cond/branch_1_fun/ppermute | solution.py:596
  55.9 10.9 %collective-permute-start.18 = (bf16[512,256]{0,1:T(8,128)(2,1)}, bf16[512,256]{0,1:T(8,128)(2,1)}, u32[]{:S(2)}, u32[]{:S(2)}) collective-permute-start(bf16[512,256]{0,1:T(8,128)(2,1)} %bitcast.24), channel_id=1, source_target_pairs={{0,4},{4,0},{1,5},{5,1},{2,6},{6,2},{3,7},{7,3},{8,12},{12,8},{9,1... | collective-permute-start | bytes 786440 | tf_op jit(solution)/shard_map/cond/branch_1_fun/ppermute | solution.py:592
  56.2 12.8 %collective-permute-start.17 = (bf16[512,256]{0,1:T(8,128)(2,1)}, bf16[512,256]{0,1:T(8,128)(2,1)}, u32[]{:S(2)}, u32[]{:S(2)}) collective-permute-start(bf16[512,256]{0,1:T(8,128)(2,1)} %bitcast.24), channel_id=1, source_target_pairs={{0,8},{8,0},{16,24},{24,16},{1,9},{9,1},{17,25},{25,17},{2,10},{10... | collective-permute-start | bytes 786440 | tf_op jit(solution)/shard_map/cond/branch_1_fun/ppermute | solution.py:596
  190.3 370.4 %all-reduce.16.cloned.1.call-start = ((), (), s32[]{:S(2)}) async-start(), calls=%async_computation.3 | async-start | bytes 12582912 | tf_op jit(solution)/shard_map/cond/branch_1_fun/psum | solution.py:738
  311.6 16.1 %collective-permute-start.36 = (bf16[512,256]{1,0:T(8,128)(2,1)S(1)}, bf16[512,256]{1,0:T(8,128)(2,1)S(1)}, u32[]{:S(2)}, u32[]{:S(2)}) collective-permute-start(bf16[512,256]{1,0:T(8,128)(2,1)S(1)} %get-tuple-element.408), channel_id=1, source_target_pairs={{0,8},{8,0},{16,24},{24,16},{1,9},{9,1},{17,25},{25,17},{2,10},{10... | collective-permute-start | bytes 786440 | tf_op jit(solution)/shard_map/cond/branch_1_fun/ppermute | solution.py:596
  313.0 12.5 %collective-permute-start.40 = (bf16[512,256]{1,0:T(8,128)(2,1)S(1)}, bf16[512,256]{1,0:T(8,128)(2,1)S(1)}, u32[]{:S(2)}, u32[]{:S(2)}) collective-permute-start(bf16[512,256]{1,0:T(8,128)(2,1)S(1)} %get-tuple-element.411), channel_id=1, source_target_pairs={{0,8},{8,0},{16,24},{24,16},{1,9},{9,1},{17,25},{25,17},{2,10},{10... | collective-permute-start | bytes 786440 | tf_op jit(solution)/shard_map/cond/branch_1_fun/ppermute | solution.py:596
  313.1 13.2 %collective-permute-start.24 = (bf16[64,2048]{1,0:T(8,128)(2,1)S(1)}, bf16[64,2048]{1,0:T(8,128)(2,1)S(1)}, u32[]{:S(2)}, u32[]{:S(2)}) collective-permute-start(bf16[64,2048]{1,0:T(8,128)(2,1)S(1)} %slice.141), channel_id=1, source_target_pairs={{3,2},{0,1},{7,6},{4,5},{11,10},{8,9},{15,14},{12,13},{19,18},{16,... | collective-permute-start | bytes 786440 | tf_op jit(solution)/shard_map/cond/branch_1_fun/ppermute | solution.py:507
  317.5 18.1 %collective-permute-start.38 = (bf16[512,256]{1,0:T(8,128)(2,1)S(1)}, bf16[512,256]{1,0:T(8,128)(2,1)S(1)}, u32[]{:S(2)}, u32[]{:S(2)}) collective-permute-start(bf16[512,256]{1,0:T(8,128)(2,1)S(1)} %add_convert_fusion.11), channel_id=1, source_target_pairs={{0,4},{4,0},{1,5},{5,1},{2,6},{6,2},{3,7},{7,3},{8,12},{12,8},{9,1... | collective-permute-start | bytes 786440 | tf_op jit(solution)/shard_map/cond/branch_1_fun/ppermute | solution.py:592
  325.4 15.7 %collective-permute-start.39 = (bf16[512,256]{1,0:T(8,128)(2,1)}, bf16[512,256]{1,0:T(8,128)(2,1)}, u32[]{:S(2)}, u32[]{:S(2)}) collective-permute-start(bf16[512,256]{1,0:T(8,128)(2,1)} %get-tuple-element.410), channel_id=1, source_target_pairs={{0,8},{8,0},{16,24},{24,16},{1,9},{9,1},{17,25},{25,17},{2,10},{10... | collective-permute-start | bytes 786440 | tf_op jit(solution)/shard_map/cond/branch_1_fun/ppermute | solution.py:596
  326.2 16.4 %collective-permute-start.41 = (bf16[512,256]{1,0:T(8,128)(2,1)}, bf16[512,256]{1,0:T(8,128)(2,1)}, u32[]{:S(2)}, u32[]{:S(2)}) collective-permute-start(bf16[512,256]{1,0:T(8,128)(2,1)} %add_convert_fusion.10), channel_id=1, source_target_pairs={{0,4},{4,0},{1,5},{5,1},{2,6},{6,2},{3,7},{7,3},{8,12},{12,8},{9,1... | collective-permute-start | bytes 786440 | tf_op jit(solution)/shard_map/cond/branch_1_fun/ppermute | solution.py:592
  326.3 12.2 %collective-permute-start.25 = (bf16[64,2048]{1,0:T(8,128)(2,1)S(1)}, bf16[64,2048]{1,0:T(8,128)(2,1)}, u32[]{:S(2)}, u32[]{:S(2)}) collective-permute-start(bf16[64,2048]{1,0:T(8,128)(2,1)S(1)} %collective-permute-done.24), channel_id=1, source_target_pairs={{2,1},{1,2},{6,5},{5,6},{10,9},{9,10},{14,13},{13,14},{18,17},{17,... | collective-permute-start | bytes 786440 | tf_op jit(solution)/shard_map/cond/branch_1_fun/ppermute | solution.py:507
  338.5 13.4 %collective-permute-start.26 = (bf16[64,2048]{1,0:T(8,128)(2,1)}, bf16[64,2048]{1,0:T(8,128)(2,1)S(1)}, u32[]{:S(2)}, u32[]{:S(2)}) collective-permute-start(bf16[64,2048]{1,0:T(8,128)(2,1)} %collective-permute-done.25), channel_id=1, source_target_pairs={{1,0},{2,3},{5,4},{6,7},{9,8},{10,11},{13,12},{14,15},{17,16},{18,... | collective-permute-start | bytes 786440 | tf_op jit(solution)/shard_map/cond/branch_1_fun/ppermute | solution.py:507
  352.8 11.3 %collective-permute-start.27 = (bf16[64,2048]{1,0:T(8,128)(2,1)S(1)}, bf16[64,2048]{1,0:T(8,128)(2,1)}, u32[]{:S(2)}, u32[]{:S(2)}) collective-permute-start(bf16[64,2048]{1,0:T(8,128)(2,1)S(1)} %get-tuple-element.419), channel_id=1, source_target_pairs={{3,2},{0,1},{7,6},{4,5},{11,10},{8,9},{15,14},{12,13},{19,18},{16,... | collective-permute-start | bytes 786440 | tf_op jit(solution)/shard_map/cond/branch_1_fun/ppermute | solution.py:507
  362.2 11.9 %collective-permute-start.33 = (bf16[64,2048]{1,0:T(8,128)(2,1)}, bf16[64,2048]{1,0:T(8,128)(2,1)}, u32[]{:S(2)}, u32[]{:S(2)}) collective-permute-start(bf16[64,2048]{1,0:T(8,128)(2,1)} %get-tuple-element.416), channel_id=1, source_target_pairs={{3,2},{0,1},{7,6},{4,5},{11,10},{8,9},{15,14},{12,13},{19,18},{16,... | collective-permute-start | bytes 786440 | tf_op jit(solution)/shard_map/cond/branch_1_fun/ppermute | solution.py:507
  364.2 11.3 %collective-permute-start.28 = (bf16[64,2048]{1,0:T(8,128)(2,1)}, bf16[64,2048]{1,0:T(8,128)(2,1)}, u32[]{:S(2)}, u32[]{:S(2)}) collective-permute-start(bf16[64,2048]{1,0:T(8,128)(2,1)} %collective-permute-done.27), channel_id=1, source_target_pairs={{2,1},{1,2},{6,5},{5,6},{10,9},{9,10},{14,13},{13,14},{18,17},{17,... | collective-permute-start | bytes 786440 | tf_op jit(solution)/shard_map/cond/branch_1_fun/ppermute | solution.py:507
  369.7 82.4 %collective-permute-start.31 = (bf16[64,2048]{1,0:T(8,128)(2,1)}, bf16[64,2048]{1,0:T(8,128)(2,1)}, u32[]{:S(2)}, u32[]{:S(2)}) collective-permute-start(bf16[64,2048]{1,0:T(8,128)(2,1)} %collective-permute-done.30), channel_id=1, source_target_pairs={{2,1},{1,2},{6,5},{5,6},{10,9},{9,10},{14,13},{13,14},{18,17},{17,... | collective-permute-start | bytes 786440 | tf_op jit(solution)/shard_map/cond/branch_1_fun/ppermute | solution.py:507
  374.1 79.3 %collective-permute-start.34 = (bf16[64,2048]{1,0:T(8,128)(2,1)}, bf16[64,2048]{1,0:T(8,128)(2,1)}, u32[]{:S(2)}, u32[]{:S(2)}) collective-permute-start(bf16[64,2048]{1,0:T(8,128)(2,1)} %collective-permute-done.33), channel_id=1, source_target_pairs={{2,1},{1,2},{6,5},{5,6},{10,9},{9,10},{14,13},{13,14},{18,17},{17,... | collective-permute-start | bytes 786440 | tf_op jit(solution)/shard_map/cond/branch_1_fun/ppermute | solution.py:507
  375.4 79.3 %collective-permute-start.29 = (bf16[64,2048]{1,0:T(8,128)(2,1)}, bf16[64,2048]{1,0:T(8,128)(2,1)}, u32[]{:S(2)}, u32[]{:S(2)}) collective-permute-start(bf16[64,2048]{1,0:T(8,128)(2,1)} %collective-permute-done.28), channel_id=1, source_target_pairs={{1,0},{2,3},{5,4},{6,7},{9,8},{10,11},{13,12},{14,15},{17,16},{18,... | collective-permute-start | bytes 786440 | tf_op jit(solution)/shard_map/cond/branch_1_fun/ppermute | solution.py:507
  453.4 10.1 %collective-permute-start.35 = (bf16[64,2048]{1,0:T(8,128)(2,1)}, bf16[64,2048]{1,0:T(8,128)(2,1)}, u32[]{:S(2)}, u32[]{:S(2)}) collective-permute-start(bf16[64,2048]{1,0:T(8,128)(2,1)} %collective-permute-done.34), channel_id=1, source_target_pairs={{1,0},{2,3},{5,4},{6,7},{9,8},{10,11},{13,12},{14,15},{17,16},{18,... | collective-permute-start | bytes 786440 | tf_op jit(solution)/shard_map/cond/branch_1_fun/ppermute | solution.py:507
  560.7 11.8 %collective-permute-start.42 = (bf16[512,2048]{1,0:T(8,128)(2,1)S(1)}, bf16[512,2048]{1,0:T(8,128)(2,1)S(1)}, u32[]{:S(2)}, u32[]{:S(2)}) collective-permute-start(bf16[512,2048]{1,0:T(8,128)(2,1)S(1)} %select_dynamic-update-slice_fusion.8), channel_id=1, source_target_pairs={{0,8},{8,0},{16,24},{24,16},{1,9},{9,1},{17,25},{25,17},{2,10},{10... | collective-permute-start | bytes 6291464 | tf_op jit(solution)/shard_map/cond/branch_1_fun/ppermute | solution.py:596
  (73 other events, 714.2 us)
Sparse Core Ops, SparseCore 0:
  190.5 230.8 all-reduce.13
  454.9 105.8 all-reduce.15
